TPU v7x, 128 devices: a whole 4x4x4 slice. The times are simulated.
128 devices in a mesh: row: 16 (over y, x_lo, core), col: 8 (over z, x_hi).
Axes of the slice: x: 4 (x_hi: 2, x_lo: 2; x = x_hi * 2 + x_lo), y: 4, z: 4, core: 2. Of those that a mesh axis runs over, the one named last changes fastest.
Arguments:
- pair: bfloat16 [2048, 2048, 128], P('row', 'col'), may hold values from -6 to 6
- counts: int32 [16, 128], replicated, may hold values from 1 to 24, 1024 in all within a row
- atom_single: bfloat16 [16384, 128], P(('row', 'col')), may hold values from -6 to 6
- w_bias: float32 [128, 4], replicated, may hold values from -24 to 24
- w_project: bfloat16 [128, 512], replicated, may hold values from -0.5 to 0.5
- w_out: bfloat16 [128, 128], replicated, may hold values from -0.5 to 0.5
- w_trans_in: bfloat16 [128, 512], replicated, may hold values from -0.5 to 0.5
- w_trans_out: bfloat16 [256, 128], replicated, may hold values from -0.375 to 0.375
- w_token: bfloat16 [128, 384], replicated, may hold values from -0.5 to 0.5
- w_row: bfloat16 [384, 128], replicated, may hold values from -0.3125 to 0.3125
- w_col: bfloat16 [384, 128], replicated, may hold values from -0.3125 to 0.3125
Outputs:
- atom_out: bfloat16 [16384, 128], P(('row', 'col'))
- token_single: bfloat16 [2048, 384], P('row')
- new_pair: bfloat16 [2048, 2048, 128], P('row', 'col')
Inputs may be any that keep to these rules, and one draw needn't show every extreme that they name: Each row of counts sums to 1024, so the atoms of row group r belong to tokens r * 128 to r * 128 + 127.
All inputs are finite; a program needn't handle non-finite values.
Results may differ from a plain program's by a relative error of at most 0.017.
Values may be sent and summed in bfloat16 or wider, within the bound.
A program may use at most 64 MiB of HBM per device.

v0:
```python
import jax
import jax.numpy as jnp
from jax import lax
from jax.sharding import PartitionSpec as P

Q_WIN = 32
K_WIN = 128


def extended(value, sides, width):
    for axis, dim in sides:
        peers, length = (lax.axis_size(axis), value.shape[dim])
        up = [(i, (i + 1) % peers) for i in range(peers - 1)]
        down = [(j, i) for i, j in up]
        last = lax.slice_in_dim(value, length - width, length, axis=dim)
        first = lax.slice_in_dim(value, 0, width, axis=dim)
        before = lax.ppermute(last, axis, up)
        after = lax.ppermute(first, axis, down)
        value = jnp.concatenate([before, value, after], axis=dim)
    return value


def normalize(values):
    values = values.astype(jnp.float32)
    average = jnp.mean(values, -1, keepdims=True)
    centred = values - average
    spread = jnp.mean(centred * centred, -1, keepdims=True)
    return centred * lax.rsqrt(spread + 1e-05)


def window_keys(rimmed, windows):
    shaped = rimmed.reshape((windows + K_WIN // Q_WIN - 1, Q_WIN) + rimmed.shape[1:])
    return jnp.concatenate(
        [shaped[offset : offset + windows] for offset in range(K_WIN // Q_WIN)], axis=1
    )


def shards(
    pair,
    counts,
    atom_single,
    w_bias,
    w_project,
    w_out,
    w_trans_in,
    w_trans_out,
    w_token,
    w_row,
    w_col,
):
    f32 = jnp.float32
    bf16 = jnp.bfloat16
    tok_row = pair.shape[0]
    tok_col = pair.shape[1]
    atom_dev, atom_width = atom_single.shape
    head_count = w_bias.shape[1]
    head_dim = atom_width // head_count
    n_col = lax.axis_size("col")
    n_row = lax.axis_size("row")
    row_id = lax.axis_index("row")
    col_id = lax.axis_index("col")
    margin = (K_WIN - Q_WIN) // 2
    windows = atom_dev // Q_WIN
    first_atom = (row_id * n_col + col_id) * atom_dev
    normed = normalize(pair)
    local_bias = jnp.einsum("ijc,ch->hij", normed, w_bias, precision=lax.Precision.HIGHEST).astype(
        bf16
    )
    low_block = jnp.clip((row_id - 1) // 2, 0, n_col - 2)
    full_rows = lax.all_gather(local_bias, "col", axis=2, tiled=True)
    bias_band = lax.dynamic_slice_in_dim(full_rows, low_block * tok_col, 2 * tok_col, 2)
    band_start = low_block * tok_col
    band_width = bias_band.shape[2]
    token_ends = jnp.cumsum(counts.reshape(-1))
    positions = first_atom - margin + jnp.arange(atom_dev + 2 * margin, dtype=jnp.int32)
    in_range = (positions >= 0) & (positions < n_row * n_col * atom_dev)
    token_ext = jnp.sum((token_ends[None, :] <= positions[:, None]).astype(jnp.int32), axis=1)
    token_query = token_ext[margin : margin + atom_dev]
    atom_norm = normalize(atom_single).astype(bf16)
    projected = jnp.dot(atom_norm, w_project, preferred_element_type=f32)
    queries = (projected[:, :atom_width] * head_dim ** (-0.5)).astype(bf16)
    keyval = projected[:, atom_width : 3 * atom_width].astype(bf16)
    gate_part = projected[:, 3 * atom_width :].astype(bf16)
    rimmed = extended(keyval, ((("row", "col"), 0),), margin)
    keys_win = window_keys(rimmed, windows)
    tokens_win = window_keys(token_ext, windows)
    range_win = window_keys(in_range, windows)
    query_local = (token_query - row_id * tok_row).reshape(windows, Q_WIN)
    query_onehot = (
        query_local[:, :, None] == jnp.arange(tok_row, dtype=jnp.int32)[None, None, :]
    ).astype(bf16)
    key_local = tokens_win - band_start
    key_onehot = (
        key_local[:, :, None] == jnp.arange(band_width, dtype=jnp.int32)[None, None, :]
    ).astype(bf16)
    picked_rows = jnp.einsum(
        "wqi,hij->whqj", query_onehot, bias_band, preferred_element_type=f32
    ).astype(bf16)
    picked = jnp.einsum("whqj,wkj->whqk", picked_rows, key_onehot, preferred_element_type=f32)
    q_heads = queries.reshape(windows, Q_WIN, head_count, head_dim)
    k_heads = keys_win[..., :atom_width].reshape(windows, K_WIN, head_count, head_dim)
    v_heads = keys_win[..., atom_width:].reshape(windows, K_WIN, head_count, head_dim)
    scores = jnp.einsum("wqhd,wkhd->whqk", q_heads, k_heads, preferred_element_type=f32) + picked
    scores = jnp.where(range_win[:, None, None, :], scores, -jnp.inf)
    row_max = jnp.max(scores, -1, keepdims=True)
    exponent = jnp.exp(scores - row_max)
    weights = (exponent / jnp.sum(exponent, -1, keepdims=True)).astype(bf16)
    attended = jnp.einsum("whqk,wkhd->wqhd", weights, v_heads, preferred_element_type=f32)
    gated = (attended.reshape(atom_dev, atom_width) * jax.nn.sigmoid(gate_part.astype(f32))).astype(
        bf16
    )
    residual = (atom_single.astype(f32) + jnp.dot(gated, w_out, preferred_element_type=f32)).astype(
        bf16
    )
    second = normalize(residual).astype(bf16)
    doubled = jnp.dot(second, w_trans_in, preferred_element_type=f32)
    hidden = (jax.nn.silu(doubled[:, : 2 * atom_width]) * doubled[:, 2 * atom_width :]).astype(bf16)
    atom_out = (
        residual.astype(f32) + jnp.dot(hidden, w_trans_out, preferred_element_type=f32)
    ).astype(bf16)
    emitted = jax.nn.relu(jnp.dot(atom_out, w_token, preferred_element_type=f32)).astype(bf16)
    local_token = token_query - row_id * tok_row
    onehot = (local_token[:, None] == jnp.arange(tok_row, dtype=jnp.int32)[None, :]).astype(bf16)
    partial_value = jnp.einsum("at,ac->tc", onehot, emitted, preferred_element_type=f32)
    totals = lax.psum(partial_value.astype(jnp.bfloat16), "col").astype(jnp.float32)
    row_counts = lax.dynamic_slice_in_dim(counts, row_id, 1, 0).reshape(tok_row)
    token_single = (totals / row_counts[:, None].astype(f32)).astype(bf16)
    row_term = jnp.dot(token_single, w_row, preferred_element_type=f32)
    all_single = lax.all_gather(token_single, "row", axis=0, tiled=True)
    col_single = lax.dynamic_slice_in_dim(all_single, col_id * tok_col, tok_col, 0)
    col_term = jnp.dot(col_single, w_col, preferred_element_type=f32)
    new_pair = (pair.astype(f32) + row_term[:, None, :] + col_term[None, :, :]).astype(bf16)
    return (atom_out, token_single, new_pair)


def solution(mesh):
    return jax.shard_map(
        shards,
        mesh=mesh,
        in_specs=(
            P("row", "col", None),
            P(),
            P(("row", "col"), None),
            P(),
            P(),
            P(),
            P(),
            P(),
            P(),
            P(),
            P(),
        ),
        out_specs=(P(("row", "col"), None), P("row", None), P("row", "col", None)),
        check_vma=False,
    )
```

profile of v0, /device:TPU:18, one launch (start us, length us, event | category | flops | bytes accessed | tf_op | source)
XLA Modules:
  0.0 239.4 jit_solution(11755029734660428189)
XLA Ops:
  7.2 0.0 all-gather.3.cloned.1.call-start
  7.2 5.8 %convert_reduce_fusion = f32[128,256]{1,0:T(8,128)S(1)} fusion(bf16[128,256,128]{2,1,0:T(8,128)(2,1)} %param.11), kind=kLoop, calls=%fused_computation.3 | loop fusion | flops 8355840 | bytes 8519680 | tf_op jit(solution)/shard_map/reduce_sum | solution.py:25
  13.1 10.9 %fusion.3 = f32[128,256]{1,0:T(8,128)S(1)} fusion(bf16[128,256,128]{2,1,0:T(8,128)(2,1)} %param.11, f32[128,256]{1,0:T(8,128)S(1)} %broadcast_multiply_fusion), kind=kLoop, calls=%fused_computation.6 | loop fusion | flops 16744448 | bytes 8650752 | tf_op jit(solution)/shard_map/reduce_sum | solution.py:27
  24.1 22.6 %fusion.19 = bf16[4,128,256]{2,0,1:T(4,128)(2,1)S(1)} fusion(bf16[128,256,128]{2,1,0:T(8,128)(2,1)S(1)} %bitcast.54, f32[128,256]{1,0:T(8,128)S(1)} %add_rsqrt_fusion, f32[128,256]{1,0:T(8,128)S(1)} %broadcast_multiply_fusion, f32[128,4]{0,1:T(4,128)S(1)} %copy-done.9), kind=kOutput, calls=%fused_computation.22 | convolution fusion | flops 214040576 | bytes 8914944 | tf_op jit(solution)/shard_map/ijc,ch->hij/dot_general | solution.py:66
  46.8 0.7 copy.32
  47.5 0.0 all-gather.3.cloned.1.call-update
  47.5 0.0 all-reduce.2.cloned.1.call-start
  47.6 0.1 copy.28
  47.8 0.2 fusion.79
  48.0 4.0 %collective-permute-start = (bf16[48,256]{1,0:T(8,128)(2,1)S(1)}, bf16[48,256]{1,0:T(8,128)(2,1)S(1)}, u32[]{:S(2)}, u32[]{:S(2)}) collective-permute-start(bf16[48,256]{1,0:T(8,128)(2,1)S(1)} %get-tuple-element.14), channel_id=1, source_target_pairs={{0,1},{1,2},{2,3},{3,4},{4,5},{5,6},{6,7},{7,8},{8,9},{9,10},{10,1... | collective-permute-start | bytes 73736 | tf_op jit(solution)/shard_map/ppermute | solution.py:17
  52.1 4.2 %collective-permute-start.1 = (bf16[48,256]{1,0:T(8,128)(2,1)S(1)}, bf16[48,256]{1,0:T(8,128)(2,1)S(1)}, u32[]{:S(2)}, u32[]{:S(2)}) collective-permute-start(bf16[48,256]{1,0:T(8,128)(2,1)S(1)} %get-tuple-element.15), channel_id=1, source_target_pairs={{1,0},{2,1},{3,2},{4,3},{5,4},{6,5},{7,6},{8,7},{9,8},{10,9},{11,1... | collective-permute-start | bytes 73736 | tf_op jit(solution)/shard_map/ppermute | solution.py:18
  56.3 0.3 reduce-window.9
  56.6 0.1 slice.175
  56.7 0.1 slice_reduce_fusion
  56.8 0.1 add_bitcast_fusion
  56.9 0.3 convert_reduce_fusion.1
  57.2 0.1 slice_subtract_fusion
  57.3 0.1 concatenate.37
  57.4 0.1 concatenate.36
  57.5 0.1 concatenate.35
  57.6 0.1 concatenate.34
  57.7 0.1 add_subtract_fusion
  57.8 0.1 pad_add_fusion
  57.9 0.1 sub.76
  58.0 0.1 reshape.192
  58.1 1.2 collective-permute-done.1
  59.4 0.1 copy.30
  59.5 0.1 copy.29
  59.7 0.2 fusion.36
  59.8 43.7 %all-gather.3.cloned.1.call-done = bf16[4,128,2048]{2,1,0:T(8,128)(2,1)} async-done(((bf16[4,128,256]{2,1,0:T(8,128)(2,1)}), bf16[4,128,2048]{2,1,0:T(8,128)(2,1)}) %all-gather.3.cloned.1.call-update) | async-done | bytes 2097168 | tf_op jit(solution)/shard_map/all_gather | solution.py:70
  103.5 1.6 fusion.18
  105.2 0.2 fusion.80
  105.4 1.0 convolution_bitcast_fusion
  106.4 0.2 copy.33
  106.5 0.2 reshape.195
  106.7 0.2 fusion.81
  107.0 0.2 fusion.51
  107.2 0.2 fusion.25
  107.5 1.0 convolution_convert_fusion.1
  108.5 0.0 all-reduce.2.cloned.1.call-update
  108.5 0.0 all-gather.5.cloned.1.call-start
  108.6 80.5 %all-reduce.2.cloned.1.call-done = bf16[128,384]{1,0:T(8,128)(2,1)} async-done(((bf16[128,384]{1,0:T(8,128)(2,1)}), bf16[128,384]{1,0:T(8,128)(2,1)}) %all-reduce.2.cloned.1.call-update) | async-done | bytes 98320 | tf_op jit(solution)/shard_map/psum | solution.py:125
  189.1 1.6 divide_convert_fusion.1
  190.7 0.7 copy.35
  191.4 1.1 fusion.82
  192.5 28.8 %all-gather.5.cloned.1.call-done = bf16[2048,384]{1,0:T(8,128)(2,1)} async-done(((bf16[128,384]{1,0:T(8,128)(2,1)}), bf16[2048,384]{1,0:T(8,128)(2,1)}) %all-gather.5.cloned.1.call-update) | async-done | bytes 1572880 | tf_op jit(solution)/shard_map/all_gather | solution.py:129
  221.3 1.1 fusion.33
  222.4 10.4 %fusion.7 = bf16[128,256,128]{2,1,0:T(8,128)(2,1)} fusion(bf16[128,256,128]{2,1,0:T(8,128)(2,1)} %param.11, f32[256,128]{1,0:T(8,128)S(1)} %fusion.33, f32[128,128]{1,0:T(8,128)S(1)} %fusion.82), kind=kLoop, calls=%fused_computation.9 | loop fusion | flops 16777216 | bytes 16973824 | tf_op jit(solution)/shard_map/convert_element_type | solution.py:132
  (47 shorter events, 0.5 us)
Async XLA Ops:
  7.2 40.6 %copy-start = (bf16[128,512]{1,0:T(8,128)(2,1)S(1)}, bf16[128,512]{1,0:T(8,128)(2,1)}, u32[]{:S(2)}) copy-start(bf16[128,512]{1,0:T(8,128)(2,1)} %param.15) | copy-start | bytes 393220
  7.2 16.8 %copy-start.9 = (f32[128,4]{0,1:T(4,128)S(1)}, f32[128,4]{0,1:T(4,128)}, u32[]{:S(2)}) copy-start(f32[128,4]{0,1:T(4,128)} %param.14) | copy-start | bytes 6148
  7.2 96.3 %all-gather.3.cloned.1.call-start = ((), (), s32[]{:S(2)}) async-start(), calls=%async_computation | async-start | bytes 2359296 | tf_op jit(solution)/shard_map/all_gather | solution.py:70
  7.2 16.8 %slice-start = ((s8[8388608]{0:T(1024)(128)(4,1)}), s8[4194304]{0:T(1024)(128)(4,1)S(1)}, s32[]{:S(2)}) async-start(s8[8388608]{0:T(1024)(128)(4,1)} %bitcast.53), calls=%async_computation.3 | async-start | bytes 8388608
  13.1 10.9 %slice-start.1 = ((s8[8388608]{0:T(1024)(128)(4,1)}), s8[4194304]{0:T(1024)(128)(4,1)S(1)}, s32[]{:S(2)}) async-start(s8[8388608]{0:T(1024)(128)(4,1)} %bitcast.53), calls=%async_computation.4 | async-start | bytes 8388608
  24.0 23.5 %copy-start.5 = (bf16[128,128]{1,0:T(8,128)(2,1)S(1)}, bf16[128,128]{1,0:T(8,128)(2,1)}, u32[]{:S(2)}) copy-start(bf16[128,128]{1,0:T(8,128)(2,1)} %param.13) | copy-start | bytes 98308
  24.0 32.3 %copy-start.6 = (s32[16,128]{1,0:T(8,128)S(1)}, s32[16,128]{1,0:T(8,128)}, u32[]{:S(2)}) copy-start(s32[16,128]{1,0:T(8,128)} %param.12) | copy-start | bytes 24580
  24.1 82.6 %copy-start.8 = (bf16[128,128]{1,0:T(8,128)(2,1)S(1)}, bf16[128,128]{1,0:T(8,128)(2,1)}, u32[]{:S(2)}) copy-start(bf16[128,128]{1,0:T(8,128)(2,1)} %param.16) | copy-start | bytes 98308
  46.7 60.3 %copy-start.1 = (bf16[128,512]{1,0:T(8,128)(2,1)S(1)}, bf16[128,512]{1,0:T(8,128)(2,1)}, u32[]{:S(2)}) copy-start(bf16[128,512]{1,0:T(8,128)(2,1)} %param.17) | copy-start | bytes 393220
  46.7 60.5 %copy-start.7 = (bf16[256,128]{1,0:T(8,128)(2,1)S(1)}, bf16[256,128]{1,0:T(8,128)(2,1)}, u32[]{:S(2)}) copy-start(bf16[256,128]{1,0:T(8,128)(2,1)} %param.18) | copy-start | bytes 196612
  46.7 60.7 %copy-start.2 = (bf16[128,384]{1,0:T(8,128)(2,1)S(1)}, bf16[128,384]{1,0:T(8,128)(2,1)}, u32[]{:S(2)}) copy-start(bf16[128,384]{1,0:T(8,128)(2,1)} %param.19) | copy-start | bytes 294916
  46.7 144.7 %copy-start.3 = (bf16[384,128]{1,0:T(8,128)(2,1)S(1)}, bf16[384,128]{1,0:T(8,128)(2,1)}, u32[]{:S(2)}) copy-start(bf16[384,128]{1,0:T(8,128)(2,1)} %param.20) | copy-start | bytes 294916
  46.7 174.5 %copy-start.4 = (bf16[384,128]{1,0:T(8,128)(2,1)S(1)}, bf16[384,128]{1,0:T(8,128)(2,1)}, u32[]{:S(2)}) copy-start(bf16[384,128]{1,0:T(8,128)(2,1)} %param.21) | copy-start | bytes 294916
  47.5 141.5 %all-reduce.2.cloned.1.call-start = ((), (), s32[]{:S(2)}) async-start(), calls=%async_computation.1 | async-start | bytes 196608 | tf_op jit(solution)/shard_map/psum | solution.py:125
  48.0 10.1 %collective-permute-start = (bf16[48,256]{1,0:T(8,128)(2,1)S(1)}, bf16[48,256]{1,0:T(8,128)(2,1)S(1)}, u32[]{:S(2)}, u32[]{:S(2)}) collective-permute-start(bf16[48,256]{1,0:T(8,128)(2,1)S(1)} %get-tuple-element.14), channel_id=1, source_target_pairs={{0,1},{1,2},{2,3},{3,4},{4,5},{5,6},{6,7},{7,8},{8,9},{9,10},{10,1... | collective-permute-start | bytes 73736 | tf_op jit(solution)/shard_map/ppermute | solution.py:17
  52.1 7.2 %collective-permute-start.1 = (bf16[48,256]{1,0:T(8,128)(2,1)S(1)}, bf16[48,256]{1,0:T(8,128)(2,1)S(1)}, u32[]{:S(2)}, u32[]{:S(2)}) collective-permute-start(bf16[48,256]{1,0:T(8,128)(2,1)S(1)} %get-tuple-element.15), channel_id=1, source_target_pairs={{1,0},{2,1},{3,2},{4,3},{5,4},{6,5},{7,6},{8,7},{9,8},{10,9},{11,1... | collective-permute-start | bytes 73736 | tf_op jit(solution)/shard_map/ppermute | solution.py:18
  108.5 112.8 %all-gather.5.cloned.1.call-start = ((), (), s32[]{:S(2)}) async-start(), calls=%async_computation.2 | async-start | bytes 1671168 | tf_op jit(solution)/shard_map/all_gather | solution.py:129
Sparse Core Ops, SparseCore 0:
  47.6 55.8 all-gather.2
  108.6 80.4 all-reduce.1
  191.5 29.7 all-gather.4
where the time goes:
time: 242 us; the launch traced here: 239 us
  waiting for transfers between devices  154 us (64%)
  other arithmetic  30.2 us (12%)
  matrix products  29.4 us (12%)
  between operations  14.2 us (6%)
  starting transfers between devices  8.36 us (3%)
  local copies, waits for them, and re-layouts  3.01 us (1%)
    psum x1, waiting for transfers between devices, shards(): lax.psum(partial_value.astype(jnp.bfloat16), 'col').astype(jnp.float32)  80.5 us
    all_gather x1, waiting for transfers between devices, shards(): full_rows = lax.all_gather(local_bias, 'col', axis=2, tiled=True)  43.7 us
    all_gather x1, waiting for transfers between devices, shards(): all_single = lax.all_gather(token_single, 'row', axis=0, tiled=True)  28.8 us
    dot_general x1, matrix products, shards(): jnp.einsum('ijc,ch->hij', normed, w_bias, precision=lax.Precision.HIGHEST)  22.6 us
    reduce_sum x3, other arithmetic, normalize(): spread = jnp.mean(centred * centred, -1, keepdims=True)  10.9 us
    convert_element_type x1, other arithmetic, shards(): (pair.astype(f32) + row_term[:, None, :] + col_term[None, :, :]).astype(b...  10.4 us
    reduce_sum x2, other arithmetic, normalize(): average = jnp.mean(values, -1, keepdims=True)  5.83 us
  transfers between devices with their start and end apart: 5, of which 4 were waited for; matrix products, arithmetic and copies ran while one was open for 2% of the time, Pallas kernels for 0%

commit v1 on v0

v1 whole, which is shorter than its diff:
```python
import functools

import jax
import jax.numpy as jnp
from jax import lax
from jax.experimental import pallas as pl
from jax.experimental.pallas import tpu as pltpu
from jax.sharding import PartitionSpec as P

MESH = pl.DeviceIdType.MESH
F32 = jnp.float32
BF16 = jnp.bfloat16
N_ROW, N_COL = 16, 8
TOK = 128
CH = 128
HEADS = 4
WIN = 32
KEYS = 128
ATOMS = 1024
MARGIN = (KEYS - WIN) // 2
EXT = ATOMS + 2 * MARGIN
OWN = ATOMS // N_COL
STEP = 16
MASK_LANE = 56
SPLIT = 64


def nt(a, b):
    return lax.dot_general(a, b, (((1,), (1,)), ((), ())), preferred_element_type=F32)


def mm(a, b):
    return jnp.dot(a, b, preferred_element_type=F32)


def layer_norm(x):
    average = jnp.mean(x, -1, keepdims=True)
    centred = x - average
    spread = jnp.mean(centred * centred, -1, keepdims=True)
    return centred * lax.rsqrt(spread + 1e-05)


def iota(shape, axis):
    return lax.broadcasted_iota(jnp.int32, shape, axis)


def exchange_kernel(
    pair_hbm,
    atom_hbm,
    counts_hbm,
    wb_hbm,
    wp_hbm,
    wo_hbm,
    wi_hbm,
    wt_hbm,
    wk_hbm,
    wr_hbm,
    wc_hbm,
    atom_out,
    single_out,
    row_out,
    col_out,
    pair_buf,
    counts,
    wb,
    wp,
    wo,
    wi,
    wt,
    wk,
    wr,
    wc,
    stat,
    diag,
    side,
    side_in,
    atoms,
    lhs,
    rhs,
    vals,
    gate,
    gated,
    emitted,
    atom_res,
    single_buf,
    row_buf,
    col_buf,
    pair_sem,
    w_sem,
    local_sem,
    send_sem,
    recv_sem,
    side_sem,
):
    r, c = lax.axis_index("row"), lax.axis_index("col")
    odd = lax.rem(r, 2)
    home = r // 2
    is_main = c == home
    helper_col = home - 1 + 2 * odd
    has_helper = (helper_col >= 0) & (helper_col < N_COL)
    is_helper = c == helper_col
    has_prev, has_next = r > 0, r < N_ROW - 1
    side_start = pl.multiple_of((1 - odd) * TOK, TOK)
    own_start = pl.multiple_of(odd * TOK, TOK)

    def pair_copy(k):
        rows = pl.ds(k * STEP, STEP)
        return pltpu.make_async_copy(pair_hbm.at[rows], pair_buf.at[rows], pair_sem.at[k])

    def half_copy(k):
        rows = pl.ds(k * STEP, STEP)
        cols = pl.ds(side_start, TOK)
        return pltpu.make_async_copy(
            pair_hbm.at[rows, cols], pair_buf.at[rows, cols], pair_sem.at[k]
        )

    weights = [
        pltpu.make_async_copy(a, b, w_sem.at[i])
        for i, (a, b) in enumerate(
            [
                (wb_hbm, wb),
                (counts_hbm, counts),
                (wp_hbm, wp),
                (wo_hbm, wo),
                (wi_hbm, wi),
                (wt_hbm, wt),
                (wk_hbm, wk),
                (wr_hbm, wr),
                (wc_hbm, wc),
            ]
        )
    ]
    steps = TOK // STEP

    @pl.when(is_main)
    def _():
        weights[0].start()
        for k in range(steps):
            pair_copy(k).start()
        for w in weights[1:]:
            w.start()

    @pl.when(is_helper)
    def _():
        weights[0].start()
        for k in range(steps):
            half_copy(k).start()

    barrier = pltpu.get_barrier_semaphore()

    def hello(row, col):
        pl.semaphore_signal(barrier, inc=1, device_id=(row, col), device_id_type=MESH)

    @pl.when(is_main)
    def _():
        for p in range(1, N_COL):
            hello(r, lax.rem(c + p, N_COL))
        for p in range(1, N_ROW):
            hello(lax.rem(r + p, N_ROW), c)

        @pl.when(has_prev)
        def _():
            hello(r - 1, N_COL - 1)

        @pl.when(has_next)
        def _():
            hello(r + 1, 0)

    @pl.when(jnp.logical_not(is_main))
    def _():
        hello(r, home)

    @pl.when(r != 2 * c)
    def _():
        hello(2 * c, c)

    @pl.when(r != 2 * c + 1)
    def _():
        hello(2 * c + 1, c)

    to_next = (c == N_COL - 1) & has_next
    to_prev = (c == 0) & has_prev

    @pl.when(to_next)
    def _():
        hello(r + 1, (r + 1) // 2)

    @pl.when(to_prev)
    def _():
        hello(r - 1, (r - 1) // 2)

    one = lambda flag: jnp.where(flag, 1, 0)
    greetings = (
        one(is_main) * (N_COL - 1 + N_ROW - 1 + one(has_prev) + one(has_next))
        + one(jnp.logical_not(is_main))
        + one(r != 2 * c)
        + one(r != 2 * c + 1)
        + one(to_next)
        + one(to_prev)
    )
    pl.semaphore_wait(barrier, greetings)

    def atom_copy(col):
        return pltpu.make_async_remote_copy(
            src_ref=atom_hbm,
            dst_ref=atoms.at[pl.ds(MARGIN + col * OWN, OWN)],
            send_sem=send_sem.at[0],
            recv_sem=recv_sem.at[col],
            device_id=(r, home),
            device_id_type=MESH,
        )

    def edge_copy(forward, row):
        start = OWN - MARGIN if forward else 0
        return pltpu.make_async_remote_copy(
            src_ref=atom_hbm.at[pl.ds(start, MARGIN)],
            dst_ref=atoms.at[pl.ds(0 if forward else MARGIN + ATOMS, MARGIN)],
            send_sem=send_sem.at[1 if forward else 2],
            recv_sem=recv_sem.at[N_COL + (0 if forward else 1)],
            device_id=(row, row // 2),
            device_id_type=MESH,
        )

    def side_copy():
        return pltpu.make_async_remote_copy(
            src_ref=side,
            dst_ref=side_in,
            send_sem=send_sem.at[3],
            recv_sem=side_sem,
            device_id=(r, home),
            device_id_type=MESH,
        )

    @pl.when(jnp.logical_not(is_main))
    def _():
        atom_copy(c).start()

    @pl.when(to_next)
    def _():
        edge_copy(True, r + 1).start()

    @pl.when(to_prev)
    def _():
        edge_copy(False, r - 1).start()

    own_atoms = pltpu.make_async_copy(
        atom_hbm, atoms.at[pl.ds(MARGIN + c * OWN, OWN)], local_sem.at[0]
    )

    @pl.when(is_main)
    def _():
        own_atoms.start()

    lane = iota((8, TOK), 1)
    sub = iota((8, TOK), 0)
    block_of = lane // 8
    on_diag = lax.rem(lane, 8) == sub

    def bias_weights():
        w = wb[...]
        w = w - jnp.mean(w, -1, keepdims=True)
        high = w.astype(BF16)
        rest = w - high.astype(F32)
        mid = rest.astype(BF16)
        low = (rest - mid.astype(F32)).astype(BF16)
        ones = jnp.ones((1, CH), BF16)
        zeros = jnp.zeros((4, CH), BF16)
        return jnp.concatenate(
            [high, ones, zeros[:3], mid, zeros, low, zeros], axis=0
        )

    def moments(i, start, seg, w24):
        x = pair_buf[i, pl.ds(start, TOK), :]
        t = nt(w24, x)
        gram = nt(x, x)
        d = jnp.zeros((8, TOK), F32)
        for k in range(TOK // 8):
            d = jnp.where(block_of == k, gram[8 * k : 8 * k + 8], d)
        rows = pl.ds(pl.multiple_of(i * 8, 8), 8)
        stat[seg, rows, :] = t[0:8] + t[8:16] + t[16:24]
        diag[seg, rows, :] = jnp.where(on_diag, d, 0.0)

    def head_bias(seg):
        def part(ref, s):
            return ref[seg, pl.ds(s, TOK, stride=8), :]

        s1 = part(stat, 4)
        s2 = part(diag, 0)
        for s in range(1, 8):
            s2 = s2 + part(diag, s)
        near = (s1 * (1 / CH)).astype(BF16).astype(F32)
        offset = s1 * (1 / CH) - near
        moment = (s2 - 2 * near * s1) + CH * (near * near)
        spread = jnp.maximum(moment * (1 / CH) - offset * offset, 0.0)
        scale = lax.rsqrt(spread + 1e-05)
        return [(part(stat, h) * scale).astype(BF16) for h in range(HEADS)]

    @pl.when(is_helper)
    def _():
        weights[0].wait()
        w24 = bias_weights()

        @pl.loop(0, steps)
        def _(k):
            half_copy(k).wait()

            @pl.loop(0, STEP, unroll=8)
            def _(u):
                moments(k * STEP + u, side_start, 1, w24)

        for h, value in enumerate(head_bias(1)):
            side[h] = value
        side_copy().start()
        side_copy().wait_send()

    @pl.when(is_main)
    def _():
        weights[0].wait()
        w24 = bias_weights()

        @pl.loop(0, steps)
        def _(k):
            pair_copy(k).wait()

            @pl.loop(0, STEP, unroll=4)
            def _(u):
                moments(k * STEP + u, own_start, 0, w24)
                moments(k * STEP + u, side_start, 1, w24)

        for w in weights[1:]:
            w.wait()

        own_counts = counts[pl.ds(r, 1), :].astype(F32)
        prev_counts = counts[pl.ds(jnp.maximum(r - 1, 0), 1), :].astype(F32)
        next_counts = counts[pl.ds(jnp.minimum(r + 1, N_ROW - 1), 1), :].astype(F32)
        stacked = jnp.concatenate(
            [own_counts, prev_counts, next_counts, jnp.zeros((5, TOK), F32)], axis=0
        )
        upper = (iota((TOK, TOK), 0) <= iota((TOK, TOK), 1)).astype(F32).astype(BF16)
        lower = (iota((TOK, TOK), 0) >= iota((TOK, TOK), 1)).astype(F32).astype(BF16)
        stacked_low = stacked.astype(BF16)
        ends = mm(stacked_low, upper)
        starts = ends - stacked
        ends_column = nt(lower, stacked_low)[:, 0:1]
        eye = (iota((TOK, TOK), 0) == iota((TOK, TOK), 1)).astype(F32).astype(BF16)
        counts_column = nt(eye, stacked_low)[:, 0:1]
        starts_column = ends_column - counts_column
        far = 1e9
        one_lane = iota((1, TOK), 1)
        after = one_lane < SPLIT
        side_from = jnp.where(
            after,
            jnp.where(has_next, starts[2:3] + ATOMS, far),
            jnp.where(has_prev, starts[1:2] - ATOMS, far),
        )
        side_to = jnp.where(
            after,
            jnp.where(has_next, ends[2:3] + ATOMS, far),
            jnp.where(has_prev, ends[1:2] - ATOMS, far),
        )
        masked = one_lane == MASK_LANE
        low_mask = jnp.where(has_prev, far, -float(MARGIN))
        mask_from = jnp.where(has_next, low_mask, float(ATOMS))
        mask_to = jnp.where(
            has_next, jnp.where(has_prev, far, 0.0), float(ATOMS + MARGIN)
        )
        side_from = jnp.where(masked, mask_from, side_from)
        side_to = jnp.where(masked, mask_to, side_to)

        def onehot(first, count, lo, hi):
            at = (iota((count, TOK), 0) + first).astype(F32)
            return jnp.where((at >= lo) & (at < hi), 1.0, 0.0).astype(BF16)

        rhs[:, CH : CH + TOK] = onehot(-MARGIN, EXT, starts[0:1], ends[0:1])
        rhs[:, CH + TOK :] = onehot(-MARGIN, EXT, side_from, side_to)
        vals[:, CH:] = jnp.ones((EXT, CH), BF16)

        own_atoms.wait()
        for p in range(1, N_COL):
            atom_copy(lax.rem(c + p, N_COL)).wait_recv()

        @pl.when(has_prev)
        def _():
            edge_copy(True, r).wait_recv()

        @pl.when(jnp.logical_not(has_prev))
        def _():
            atoms[0:MARGIN, :] = jnp.zeros((MARGIN, CH), BF16)

        @pl.when(has_next)
        def _():
            edge_copy(False, r).wait_recv()

        @pl.when(jnp.logical_not(has_next))
        def _():
            atoms[MARGIN + ATOMS :, :] = jnp.zeros((MARGIN, CH), BF16)

        head_of = iota((WIN, CH), 1) // (CH // HEADS)
        pieces = [(0, MARGIN, False)]
        pieces += [(MARGIN + 256 * k, 256, True) for k in range(ATOMS // 256)]
        pieces += [(MARGIN + ATOMS, MARGIN, False)]
        for start, count, inside in pieces:
            span = slice(start, start + count)
            norm = layer_norm(atoms[span, :].astype(F32)).astype(BF16)
            projected = mm(norm, wp[...])
            rhs[span, 0:CH] = projected[:, CH : 2 * CH].astype(BF16)
            vals[span, 0:CH] = projected[:, 2 * CH : 3 * CH].astype(BF16)
            if inside:
                first = start - MARGIN
                gate[first : first + count, :] = projected[:, 3 * CH :]
                queries = projected[:, 0:CH] * (CH // HEADS) ** -0.5
                for w in range(count // WIN):
                    window = queries[w * WIN : (w + 1) * WIN]
                    base = (first + w * WIN) * HEADS
                    for h in range(HEADS):
                        lhs[base + h * WIN : base + (h + 1) * WIN, 0:CH] = jnp.where(
                            head_of == h, window, 0.0
                        ).astype(BF16)

        own_bias = head_bias(0)
        main_side = head_bias(1)

        @pl.when(has_helper)
        def _():
            side_copy().wait_recv()

        @pl.when(jnp.logical_not(has_helper))
        def _():
            side_in[...] = jnp.zeros((HEADS, TOK, TOK), BF16)

        side_lane = iota((TOK, TOK), 1)
        mine = (side_lane < SPLIT) == (odd == 0)
        for h in range(HEADS):
            joined = jnp.where(
                mine, main_side[h].astype(F32), side_in[h].astype(F32)
            )
            joined = jnp.where(side_lane == MASK_LANE, -1e30, joined).astype(BF16)
            both = jnp.concatenate([own_bias[h], joined], axis=1)
            for k in range(ATOMS // 256):
                first = k * 256
                picked = mm(
                    rhs[MARGIN + first : MARGIN + first + 256, CH : CH + TOK], both
                ).astype(BF16)
                for w in range(256 // WIN):
                    base = (first + w * WIN) * HEADS + h * WIN
                    lhs[base : base + WIN, CH:] = picked[w * WIN : (w + 1) * WIN]

        @pl.loop(0, ATOMS // WIN, unroll=4)
        def _(w):
            keys = pl.ds(pl.multiple_of(w * WIN, WIN), KEYS)
            rows = pl.ds(pl.multiple_of(w * WIN * HEADS, WIN * HEADS), WIN * HEADS)
            scores = nt(lhs[rows, :], rhs[keys, :])
            top = jnp.max(scores, -1, keepdims=True)
            weight = jnp.exp(scores - top).astype(BF16)
            total = mm(weight, vals[keys, :])
            above = total[0:WIN, 0:CH]
            below = total[0:WIN, CH:]
            for h in range(1, HEADS):
                here = head_of == h
                above = jnp.where(here, total[h * WIN : (h + 1) * WIN, 0:CH], above)
                below = jnp.where(here, total[h * WIN : (h + 1) * WIN, CH:], below)
            span = pl.ds(pl.multiple_of(w * WIN, WIN), WIN)
            opened = 1.0 + jnp.exp(-gate[span, :])
            gated[span, :] = (above / (below * opened)).astype(BF16)

        for k in range(ATOMS // 256):
            span = slice(k * 256, (k + 1) * 256)
            ext = slice(MARGIN + k * 256, MARGIN + (k + 1) * 256)
            residual = (atoms[ext, :].astype(F32) + mm(gated[span, :], wo[...])).astype(BF16)
            residual = residual.astype(F32)
            second = layer_norm(residual).astype(BF16)
            doubled = mm(second, wi[...])
            swish = doubled[:, 0 : 2 * CH]
            hidden = (swish / (1.0 + jnp.exp(-swish)) * doubled[:, 2 * CH :]).astype(BF16)
            out = (residual + mm(hidden, wt[...])).astype(BF16)
            atom_res[span, :] = out
            emitted[span, :] = jnp.maximum(mm(out, wk[...]), 0.0).astype(BF16)

        at = iota((TOK, ATOMS), 1).astype(F32)
        member = jnp.where((at >= starts_column) & (at < ends_column), 1.0, 0.0)
        totals = mm(member.astype(BF16), emitted[...])
        single = (totals / counts_column).astype(BF16)
        single_buf[...] = single
        row_buf[...] = mm(single, wr[...]).astype(BF16)
        col_buf[...] = mm(single, wc[...]).astype(BF16)

    def send(src, dst, slot, recv, row, col):
        return pltpu.make_async_remote_copy(
            src_ref=src,
            dst_ref=dst,
            send_sem=send_sem.at[slot],
            recv_sem=recv_sem.at[recv],
            device_id=(row, col),
            device_id_type=MESH,
        )

    base = N_COL + 2

    def row_send(p):
        return send(row_buf, row_out, 4 + p, base, r, lax.rem(c + p, N_COL))

    def single_send(p):
        return send(
            single_buf, single_out, 4 + N_COL + p, base + 1, r, lax.rem(c + p, N_COL)
        )

    def atom_send(p):
        col = lax.rem(c + p, N_COL)
        return send(
            atom_res.at[pl.ds(col * OWN, OWN)],
            atom_out,
            4 + 2 * N_COL + p,
            base + 2,
            r,
            col,
        )

    def col_send(p, parity):
        return send(
            col_buf,
            col_out.at[pl.ds(parity * TOK, TOK)],
            4 + 3 * N_COL + p,
            base + 3 + parity,
            lax.rem(r + p, N_ROW),
            c,
        )

    @pl.when(is_main)
    def _():
        for p in range(1, N_ROW):
            col_send(p, odd).start()
        for p in range(1, N_COL):
            row_send(p).start()
        for p in range(1, N_COL):
            atom_send(p).start()
        for p in range(1, N_COL):
            single_send(p).start()
        locals_ = [
            pltpu.make_async_copy(row_buf, row_out, local_sem.at[1]),
            pltpu.make_async_copy(single_buf, single_out, local_sem.at[2]),
            pltpu.make_async_copy(
                atom_res.at[pl.ds(c * OWN, OWN)], atom_out, local_sem.at[3]
            ),
            pltpu.make_async_copy(
                col_buf, col_out.at[pl.ds(odd * TOK, TOK)], local_sem.at[4]
            ),
        ]
        for copy in locals_:
            copy.start()
        for copy in locals_:
            copy.wait()
        for p in range(1, N_ROW):
            col_send(p, odd).wait_send()
        for p in range(1, N_COL):
            row_send(p).wait_send()
            atom_send(p).wait_send()
            single_send(p).wait_send()

    @pl.when(jnp.logical_not(is_main))
    def _():
        atom_copy(c).wait_send()
        row_send(1).wait_recv()
        atom_send(1).wait_recv()
        single_send(1).wait_recv()

    @pl.when(to_next)
    def _():
        edge_copy(True, r + 1).wait_send()

    @pl.when(to_prev)
    def _():
        edge_copy(False, r - 1).wait_send()

    @pl.when(r != 2 * c)
    def _():
        col_send(1, 0).wait_recv()

    @pl.when(r != 2 * c + 1)
    def _():
        col_send(1, 1).wait_recv()


def update_kernel(pair, row, col, atom, single, new_pair, atom_out, single_out):
    @pl.when(pl.program_id(0) == 0)
    def _():
        atom_out[...] = atom[...]
        single_out[...] = single[...]

    rows = pair.shape[0]
    column = col[...].astype(F32)
    for i in range(rows):
        term = row[i : i + 1, :].astype(F32)
        new_pair[i] = (pair[i].astype(F32) + (column + term)).astype(BF16)


def shards(
    pair, counts, atom_single, w_bias, w_project, w_out, w_trans_in, w_trans_out, w_token, w_row, w_col
):
    any_ = pl.BlockSpec(memory_space=pl.ANY)
    vmem = pltpu.VMEM
    weights = (w_bias.T, w_project, w_out, w_trans_in, w_trans_out, w_token, w_row, w_col)
    atom, single, row, col = pl.pallas_call(
        exchange_kernel,
        out_shape=(
            jax.ShapeDtypeStruct((OWN, CH), BF16),
            jax.ShapeDtypeStruct((TOK, 3 * CH), BF16),
            jax.ShapeDtypeStruct((TOK, CH), BF16),
            jax.ShapeDtypeStruct((2 * TOK, CH), BF16),
        ),
        in_specs=[any_] * (3 + len(weights)),
        out_specs=(any_,) * 4,
        scratch_shapes=[
            vmem((TOK, 2 * TOK, CH), BF16),
            vmem(counts.shape, jnp.int32),
            *[vmem(w.shape, w.dtype) for w in weights],
            vmem((2, 8 * TOK, TOK), F32),
            vmem((2, 8 * TOK, TOK), F32),
            vmem((HEADS, TOK, TOK), BF16),
            vmem((HEADS, TOK, TOK), BF16),
            vmem((EXT, CH), BF16),
            vmem((ATOMS * HEADS, CH + 2 * TOK), BF16),
            vmem((EXT, CH + 2 * TOK), BF16),
            vmem((EXT, 2 * CH), BF16),
            vmem((ATOMS, CH), F32),
            vmem((ATOMS, CH), BF16),
            vmem((ATOMS, 3 * CH), BF16),
            vmem((ATOMS, CH), BF16),
            vmem((TOK, 3 * CH), BF16),
            vmem((TOK, CH), BF16),
            vmem((TOK, CH), BF16),
            pltpu.SemaphoreType.DMA((TOK // STEP,)),
            pltpu.SemaphoreType.DMA((1 + len(weights),)),
            pltpu.SemaphoreType.DMA((5,)),
            pltpu.SemaphoreType.DMA((4 + 3 * N_COL + N_ROW,)),
            pltpu.SemaphoreType.DMA((N_COL + 7,)),
            pltpu.SemaphoreType.DMA,
        ],
        compiler_params=pltpu.CompilerParams(
            collective_id=0, has_side_effects=True, vmem_limit_bytes=40 * 2**20
        ),
    )(pair, atom_single, counts, *weights)
    rows = 16
    whole = lambda a: pl.BlockSpec(a.shape, lambda i: (0,) * a.ndim)
    block = pl.BlockSpec((rows,) + pair.shape[1:], lambda i: (i, 0, 0))
    new_pair, atom_out, token_single = pl.pallas_call(
        update_kernel,
        grid=(pair.shape[0] // rows,),
        out_shape=(
            jax.ShapeDtypeStruct(pair.shape, BF16),
            jax.ShapeDtypeStruct(atom.shape, BF16),
            jax.ShapeDtypeStruct(single.shape, BF16),
        ),
        in_specs=[
            block,
            pl.BlockSpec((rows, CH), lambda i: (i, 0)),
            whole(col),
            whole(atom),
            whole(single),
        ],
        out_specs=(block, whole(atom), whole(single)),
        compiler_params=pltpu.CompilerParams(vmem_limit_bytes=16 * 2**20),
    )(pair, row, col, atom, single)
    return atom_out, token_single, new_pair


def solution(mesh):
    return jax.shard_map(
        shards,
        mesh=mesh,
        in_specs=(P("row", "col", None), P(), P(("row", "col"), None)) + (P(),) * 8,
        out_specs=(P(("row", "col"), None), P("row", None), P("row", "col", None)),
        check_vma=False,
    )
```

time: 242 us -> 75.9 us (0.31)
  the two profiles are of different devices: /device:TPU:18 before, /device:TPU:12 now
where the time goes in v1:
time: 75.9 us; the launch traced here: 75.4 us
  Pallas kernels  63.1 us (83%)
  local copies, waits for them, and re-layouts  11.6 us (15%)
    pallas_call x1, Pallas kernels, shards(): pl.pallas_call(exchange_kernel, out_shape=(jax.ShapeDtypeStruct((OWN, CH)...  57.8 us
    unnamed x22, local copies, waits for them, and re-layouts  11.6 us
    pallas_call x1, Pallas kernels, shards(): pl.pallas_call(update_kernel, grid=(pair.shape[0] // rows,), out_shape=(j...  5.28 us

profile of v1, /device:TPU:12, one launch (start us, length us, event | category | flops | bytes accessed | tf_op | source)
XLA Modules:
  0.0 75.4 jit_solution(15876048870117788435)
XLA Ops:
  0.6 0.0 copy-start
  0.6 3.4 %copy-done = bf16[128,256,128]{2,1,0:T(8,128)(2,1)S(1)} copy-done((bf16[128,256,128]{2,1,0:T(8,128)(2,1)S(1)}, bf16[128,256,128]{2,1,0:T(8,128)(2,1)}, u32[]{:S(2)}) %copy-start) | copy-done | bytes 8388632
  4.0 0.0 copy-start.1
  4.0 0.9 %copy-done.1 = bf16[128,512]{1,0:T(8,128)(2,1)S(1)} copy-done((bf16[128,512]{1,0:T(8,128)(2,1)S(1)}, bf16[128,512]{1,0:T(8,128)(2,1)}, u32[]{:S(2)}) %copy-start.1) | copy-done | bytes 131096
  4.9 0.0 copy-start.2
  4.9 0.9 %copy-done.2 = bf16[128,512]{1,0:T(8,128)(2,1)S(1)} copy-done((bf16[128,512]{1,0:T(8,128)(2,1)S(1)}, bf16[128,512]{1,0:T(8,128)(2,1)}, u32[]{:S(2)}) %copy-start.2) | copy-done | bytes 131096
  5.8 0.0 copy-start.3
  5.8 0.9 %copy-done.3 = bf16[128,384]{1,0:T(8,128)(2,1)S(1)} copy-done((bf16[128,384]{1,0:T(8,128)(2,1)S(1)}, bf16[128,384]{1,0:T(8,128)(2,1)}, u32[]{:S(2)}) %copy-start.3) | copy-done | bytes 98328
  6.7 0.0 copy-start.4
  6.7 0.9 %copy-done.4 = bf16[384,128]{1,0:T(8,128)(2,1)S(1)} copy-done((bf16[384,128]{1,0:T(8,128)(2,1)S(1)}, bf16[384,128]{1,0:T(8,128)(2,1)}, u32[]{:S(2)}) %copy-start.4) | copy-done | bytes 98328
  7.6 0.0 copy-start.5
  7.6 0.9 %copy-done.5 = bf16[384,128]{1,0:T(8,128)(2,1)S(1)} copy-done((bf16[384,128]{1,0:T(8,128)(2,1)S(1)}, bf16[384,128]{1,0:T(8,128)(2,1)}, u32[]{:S(2)}) %copy-start.5) | copy-done | bytes 98328
  8.5 0.0 copy-start.6
  8.5 0.8 %copy-done.6 = bf16[256,128]{1,0:T(8,128)(2,1)S(1)} copy-done((bf16[256,128]{1,0:T(8,128)(2,1)S(1)}, bf16[256,128]{1,0:T(8,128)(2,1)}, u32[]{:S(2)}) %copy-start.6) | copy-done | bytes 65560
  9.3 0.0 copy-start.7
  9.3 0.8 %copy-done.7 = bf16[128,128]{1,0:T(8,128)(2,1)S(1)} copy-done((bf16[128,128]{1,0:T(8,128)(2,1)S(1)}, bf16[128,128]{1,0:T(8,128)(2,1)}, u32[]{:S(2)}) %copy-start.7) | copy-done | bytes 32792
  10.1 0.0 copy-start.8
  10.1 0.8 %copy-done.8 = bf16[128,128]{1,0:T(8,128)(2,1)S(1)} copy-done((bf16[128,128]{1,0:T(8,128)(2,1)S(1)}, bf16[128,128]{1,0:T(8,128)(2,1)}, u32[]{:S(2)}) %copy-start.8) | copy-done | bytes 32792
  10.9 0.0 copy-start.9
  10.9 0.7 copy-done.9
  11.6 0.0 copy-start.10
  11.6 0.7 copy-done.10
  12.2 57.8 %shard_map.130 = (bf16[128,128]{1,0:T(8,128)(2,1)S(1)}, bf16[128,384]{1,0:T(8,128)(2,1)S(1)}, bf16[128,128]{1,0:T(8,128)(2,1)S(1)}, bf16[256,128]{1,0:T(8,128)(2,1)S(1)}) custom-call(bf16[128,256,128]{2,1,0:T(8,128)(2,1)S(1)} %copy-done, bf16[128,128]{1,0:T(8,128)(2,1)S(1)} %copy-done.7, s32[16,128]{1,0:T(8,128)S(1)} %copy-done.9, f32[4,128]{1,0:T(4,128)S(1)} %bitcast.1, ...), custom_call_target="tpu_custom_call" | custom-call | tf_op jit(solution)/shard_map/pallas_call | solution.py:602
  70.1 5.3 %shard_map.131 = (bf16[128,256,128]{2,1,0:T(8,128)(2,1)}, bf16[128,128]{1,0:T(8,128)(2,1)}, bf16[128,384]{1,0:T(8,128)(2,1)}) custom-call(bf16[128,256,128]{2,1,0:T(8,128)(2,1)S(1)} %copy-done, bf16[128,128]{1,0:T(8,128)(2,1)S(1)} %get-tuple-element.10.row, bf16[256,128]{1,0:T(8,128)(2,1)S(1)} %get-tuple-element.11.col, ...), custom_call_target="tpu_custom_call" | custom-call | tf_op jit(solution)/shard_map/pallas_call | solution.py:645
Async XLA Ops:
  0.6 3.4 %copy-start = (bf16[128,256,128]{2,1,0:T(8,128)(2,1)S(1)}, bf16[128,256,128]{2,1,0:T(8,128)(2,1)}, u32[]{:S(2)}) copy-start(bf16[128,256,128]{2,1,0:T(8,128)(2,1)} %pair.1) | copy-start | bytes 25165828
  4.0 0.9 %copy-start.1 = (bf16[128,512]{1,0:T(8,128)(2,1)S(1)}, bf16[128,512]{1,0:T(8,128)(2,1)}, u32[]{:S(2)}) copy-start(bf16[128,512]{1,0:T(8,128)(2,1)} %wp_hbm.1) | copy-start | bytes 393220
  4.9 0.9 %copy-start.2 = (bf16[128,512]{1,0:T(8,128)(2,1)S(1)}, bf16[128,512]{1,0:T(8,128)(2,1)}, u32[]{:S(2)}) copy-start(bf16[128,512]{1,0:T(8,128)(2,1)} %wi_hbm.1) | copy-start | bytes 393220
  5.8 0.9 %copy-start.3 = (bf16[128,384]{1,0:T(8,128)(2,1)S(1)}, bf16[128,384]{1,0:T(8,128)(2,1)}, u32[]{:S(2)}) copy-start(bf16[128,384]{1,0:T(8,128)(2,1)} %wk_hbm.1) | copy-start | bytes 294916
  6.7 0.9 %copy-start.4 = (bf16[384,128]{1,0:T(8,128)(2,1)S(1)}, bf16[384,128]{1,0:T(8,128)(2,1)}, u32[]{:S(2)}) copy-start(bf16[384,128]{1,0:T(8,128)(2,1)} %wr_hbm.1) | copy-start | bytes 294916
  7.6 0.9 %copy-start.5 = (bf16[384,128]{1,0:T(8,128)(2,1)S(1)}, bf16[384,128]{1,0:T(8,128)(2,1)}, u32[]{:S(2)}) copy-start(bf16[384,128]{1,0:T(8,128)(2,1)} %wc_hbm.1) | copy-start | bytes 294916
  8.5 0.8 %copy-start.6 = (bf16[256,128]{1,0:T(8,128)(2,1)S(1)}, bf16[256,128]{1,0:T(8,128)(2,1)}, u32[]{:S(2)}) copy-start(bf16[256,128]{1,0:T(8,128)(2,1)} %wt_hbm.1) | copy-start | bytes 196612
  9.3 0.8 %copy-start.7 = (bf16[128,128]{1,0:T(8,128)(2,1)S(1)}, bf16[128,128]{1,0:T(8,128)(2,1)}, u32[]{:S(2)}) copy-start(bf16[128,128]{1,0:T(8,128)(2,1)} %atom_hbm.1) | copy-start | bytes 98308
  10.1 0.8 %copy-start.8 = (bf16[128,128]{1,0:T(8,128)(2,1)S(1)}, bf16[128,128]{1,0:T(8,128)(2,1)}, u32[]{:S(2)}) copy-start(bf16[128,128]{1,0:T(8,128)(2,1)} %wo_hbm.1) | copy-start | bytes 98308
  10.9 0.7 copy-start.9
  11.6 0.7 copy-start.10

commit v2 on v1

v2 whole, which is shorter than its diff:
```python
import functools

import jax
import jax.numpy as jnp
from jax import lax
from jax.experimental import pallas as pl
from jax.experimental.pallas import tpu as pltpu
from jax.sharding import PartitionSpec as P

MESH = pl.DeviceIdType.MESH
F32 = jnp.float32
BF16 = jnp.bfloat16
N_ROW, N_COL = 16, 8
TOK = 128
CH = 128
HEADS = 4
WIN = 32
KEYS = 128
ATOMS = 1024
MARGIN = (KEYS - WIN) // 2
EXT = ATOMS + 2 * MARGIN
OWN = ATOMS // N_COL
STEP = 16
REACH = 80
HALF = REACH // 2
EDGES = (0, 1, 30, 31)
MASK_LANE = 56
ATTEND_UNROLL = 14
SPLIT = 64


def nt(a, b):
    return lax.dot_general(a, b, (((1,), (1,)), ((), ())), preferred_element_type=F32)


def mm(a, b):
    return jnp.dot(a, b, preferred_element_type=F32)


def layer_norm(x):
    average = jnp.mean(x, -1, keepdims=True)
    centred = x - average
    spread = jnp.mean(centred * centred, -1, keepdims=True)
    return centred * lax.rsqrt(spread + 1e-05)


def iota(shape, axis):
    return lax.broadcasted_iota(jnp.int32, shape, axis)


def exchange_kernel(
    pair_hbm,
    atom_hbm,
    counts_hbm,
    wb_hbm,
    wp_hbm,
    wo_hbm,
    wi_hbm,
    wt_hbm,
    wk_hbm,
    wr_hbm,
    wc_hbm,
    atom_out,
    single_out,
    row_out,
    col_out,
    own_pair,
    side_pair,
    counts,
    wb,
    wp,
    wo,
    wi,
    wt,
    wk,
    wr,
    wc,
    stat,
    diag,
    side,
    side_in,
    atoms,
    queries,
    picked,
    picked_side,
    rhs,
    vals,
    gate,
    gated,
    resid,
    resid_in,
    emitted,
    member,
    own_sem,
    side_pair_sem,
    w_sem,
    local_sem,
    send_sem,
    recv_sem,
):
    r, c = lax.axis_index("row"), lax.axis_index("col")
    odd = lax.rem(r, 2)
    home = r // 2
    is_main = c == home
    not_main = jnp.logical_not(is_main)
    helper_col = home - 1 + 2 * odd
    has_helper = (helper_col >= 0) & (helper_col < N_COL)
    is_helper = c == helper_col
    has_prev, has_next = r > 0, r < N_ROW - 1
    z, x_hi = c // 2, lax.rem(c, 2)
    y, x_lo = r // 4, lax.rem(r // 2, 2)
    sibling = r + 1 - 2 * odd
    col_main = 2 * c + odd
    fed_by_main = r != col_main
    row_peers = [
        (lax.rem(z + dz, 4) * 2 + (1 - x_hi if dx else x_hi))
        for dz, dx in ((2, 1), (1, 1), (3, 1), (2, 0), (0, 1), (1, 0), (3, 0))
    ]
    col_peers = [
        (lax.rem(y + dy, 4) * 2 + (1 - x_lo if dx else x_lo)) * 2 + odd
        for dy, dx in ((2, 1), (1, 1), (3, 1), (2, 0), (1, 0), (3, 0), (0, 1))
    ]
    own_start = pl.multiple_of(odd * TOK, TOK)
    on_main_next = odd == 0
    side_is_next = on_main_next == is_main
    side_rows = jnp.where(side_is_next, TOK - REACH, 0)
    side_start = pl.multiple_of((1 - odd) * TOK + jnp.where(side_is_next, 0, SPLIT), SPLIT)

    def own_copy(k):
        rows = pl.ds(k * STEP, STEP)
        return pltpu.make_async_copy(
            pair_hbm.at[rows, pl.ds(own_start, TOK)], own_pair.at[rows], own_sem.at[k]
        )

    def side_pair_copy(k):
        return pltpu.make_async_copy(
            pair_hbm.at[pl.ds(side_rows + k * HALF, HALF), pl.ds(side_start, SPLIT)],
            side_pair.at[:, pl.ds(k * SPLIT, SPLIT)],
            side_pair_sem.at[k],
        )

    weights = [
        pltpu.make_async_copy(a, b, w_sem.at[i])
        for i, (a, b) in enumerate(
            [
                (wb_hbm, wb),
                (counts_hbm, counts),
                (wp_hbm, wp),
                (wo_hbm, wo),
                (wi_hbm, wi),
                (wt_hbm, wt),
                (wk_hbm, wk),
                (wr_hbm, wr),
                (wc_hbm, wc),
            ]
        )
    ]
    receiver_weights = [weights[4], weights[5], weights[7]]
    steps = TOK // STEP

    barrier = pltpu.get_barrier_semaphore()

    def hello(row, col):
        pl.semaphore_signal(barrier, inc=1, device_id=(row, col), device_id_type=MESH)

    to_next = (c == N_COL - 1) & has_next
    to_prev = (c == 0) & has_prev

    @pl.when(is_main)
    def _():
        for col in row_peers:
            hello(r, col)

        @pl.when(has_prev)
        def _():
            hello(r - 1, N_COL - 1)

        @pl.when(has_next)
        def _():
            hello(r + 1, 0)

        for row in col_peers:
            hello(row, c)

    @pl.when(not_main)
    def _():
        hello(r, home)

    @pl.when(fed_by_main)
    def _():
        hello(col_main, c)

    hello(sibling, c)

    @pl.when(to_next)
    def _():
        hello(r + 1, (r + 1) // 2)

    @pl.when(to_prev)
    def _():
        hello(r - 1, (r - 1) // 2)

    def one(flag):
        return jnp.where(flag, 1, 0)

    greetings = (
        1
        + one(is_main) * (2 * 7 + one(has_prev) + one(has_next))
        + one(not_main)
        + one(fed_by_main)
        + one(to_next)
        + one(to_prev)
    )

    @pl.when(is_main)
    def _():
        weights[1].start()
        weights[0].start()
        for k in range(2):
            side_pair_copy(k).start()
        for k in range(steps):
            own_copy(k).start()
        for w in weights[2:]:
            w.start()

    @pl.when(not_main)
    def _():
        @pl.when(is_helper)
        def _():
            weights[0].start()
            for k in range(2):
                side_pair_copy(k).start()

        for w in receiver_weights:
            w.start()

    def atom_copy(col):
        return pltpu.make_async_remote_copy(
            src_ref=atom_hbm,
            dst_ref=atoms.at[pl.ds(MARGIN + col * OWN, OWN)],
            send_sem=send_sem.at[0],
            recv_sem=recv_sem.at[col],
            device_id=(r, home),
            device_id_type=MESH,
        )

    def edge_copy(forward, row):
        start = OWN - MARGIN if forward else 0
        return pltpu.make_async_remote_copy(
            src_ref=atom_hbm.at[pl.ds(start, MARGIN)],
            dst_ref=atoms.at[pl.ds(0 if forward else MARGIN + ATOMS, MARGIN)],
            send_sem=send_sem.at[1 if forward else 2],
            recv_sem=recv_sem.at[N_COL + (0 if forward else 1)],
            device_id=(row, row // 2),
            device_id_type=MESH,
        )

    def side_copy():
        return pltpu.make_async_remote_copy(
            src_ref=side,
            dst_ref=side_in,
            send_sem=send_sem.at[3],
            recv_sem=recv_sem.at[N_COL + 2],
            device_id=(r, home),
            device_id_type=MESH,
        )

    own_atoms = pltpu.make_async_copy(
        atom_hbm, atoms.at[pl.ds(MARGIN + c * OWN, OWN)], local_sem.at[0]
    )

    @pl.when(is_main)
    def _():
        own_atoms.start()

    @pl.when(not_main)
    def _():
        pl.semaphore_wait(barrier, greetings)
        atom_copy(c).start()

    @pl.when(to_next & not_main)
    def _():
        edge_copy(True, r + 1).start()

    @pl.when(to_prev & not_main)
    def _():
        edge_copy(False, r - 1).start()

    lane = iota((8, TOK), 1)
    sub = iota((8, TOK), 0)
    block_of = lane // 8
    on_diag = lax.rem(lane, 8) == sub

    def bias_weights():
        w = wb[...]
        w = w - jnp.mean(w, -1, keepdims=True)
        high = w.astype(BF16)
        rest = w - high.astype(F32)
        mid = rest.astype(BF16)
        low = (rest - mid.astype(F32)).astype(BF16)
        ones = jnp.ones((1, CH), BF16)
        zeros = jnp.zeros((12, CH), BF16)
        return jnp.concatenate(
            [high, ones, zeros[:3], mid, zeros[:4], low, zeros], axis=0
        )

    def moments(x, i, first, w32):
        t = nt(jnp.concatenate([w32, x], axis=0), x)
        d = jnp.zeros((8, TOK), F32)
        for k in range(TOK // 8):
            d = jnp.where(block_of == k, t[32 + 8 * k : 40 + 8 * k], d)
        rows = pl.ds(pl.multiple_of(first + i * 8, 8), 8)
        stat[rows, :] = t[0:8] + t[8:16] + t[16:24]
        diag[rows, :] = jnp.where(on_diag, d, 0.0)

    def side_moments(w32):
        for k in range(2):
            side_pair_copy(k).wait()

        @pl.loop(0, HALF, unroll=8)
        def _(i):
            moments(side_pair[i], i, 8 * TOK, w32)

    def head_bias(first, count):
        def part(ref, s):
            return ref[pl.ds(first + s, count, stride=8), :]

        s1 = part(stat, 4)
        s2 = part(diag, 0)
        for s in range(1, 8):
            s2 = s2 + part(diag, s)
        near = (s1 * (1 / CH)).astype(BF16).astype(F32)
        offset = s1 * (1 / CH) - near
        moment = (s2 - 2 * near * s1) + CH * (near * near)
        spread = jnp.maximum(moment * (1 / CH) - offset * offset, 0.0)
        scale = lax.rsqrt(spread + 1e-05)
        return [part(stat, h) * scale for h in range(HEADS)]

    def transition(x):
        residual = x.astype(F32)
        second = layer_norm(residual).astype(BF16)
        doubled = mm(second, wi[...])
        swish = doubled[:, 0 : 2 * CH]
        hidden = swish * (0.5 + 0.5 * jnp.tanh(0.5 * swish)) * doubled[:, 2 * CH :]
        return (residual + mm(hidden.astype(BF16), wt[...])).astype(BF16)

    @pl.when(is_helper)
    def _():
        weights[0].wait()
        side_moments(bias_weights())
        for h, value in enumerate(head_bias(8 * TOK, HALF)):
            side[h] = value
        side_copy().start()
        side_copy().wait_send()

    def send(src, dst, slot, recv, row, col):
        return pltpu.make_async_remote_copy(
            src_ref=src,
            dst_ref=dst,
            send_sem=send_sem.at[slot],
            recv_sem=recv_sem.at[recv],
            device_id=(row, col),
            device_id_type=MESH,
        )

    base = N_COL + 3

    def resid_send(p):
        col = row_peers[p]
        return send(resid.at[pl.ds(col * OWN, OWN)], resid_in, 4 + p, base, r, col)

    def single_send(p):
        return send(single_out, single_out, 12 + p, base + 1, r, row_peers[p])

    own_half = col_out.at[pl.ds(pl.multiple_of(odd * TOK, TOK), TOK)]

    def col_send(p):
        return send(own_half, own_half, 20 + p, base + 2, col_peers[p], c)

    def col_forward():
        return send(own_half, own_half, 28, base + 3, sibling, c)

    @pl.when(is_main)
    def _():
        weights[1].wait()
        own_counts = counts[pl.ds(r, 1), :].astype(F32)
        prev_counts = counts[pl.ds(jnp.maximum(r - 1, 0), 1), :].astype(F32)
        next_counts = counts[pl.ds(jnp.minimum(r + 1, N_ROW - 1), 1), :].astype(F32)
        stacked = jnp.concatenate(
            [own_counts, prev_counts, next_counts, jnp.zeros((5, TOK), F32)], axis=0
        )
        upper = (iota((TOK, TOK), 0) <= iota((TOK, TOK), 1)).astype(F32).astype(BF16)
        lower = (iota((TOK, TOK), 0) >= iota((TOK, TOK), 1)).astype(F32).astype(BF16)
        stacked_low = stacked.astype(BF16)
        ends = mm(stacked_low, upper)
        starts = ends - stacked
        ends_column = nt(lower, stacked_low)[:, 0:1]
        eye = (iota((TOK, TOK), 0) == iota((TOK, TOK), 1)).astype(F32).astype(BF16)
        counts_column = nt(eye, stacked_low)[:, 0:1]
        starts_column = ends_column - counts_column
        far = 1e9
        one_lane = iota((1, TOK), 1)
        after = one_lane < SPLIT
        side_from = jnp.where(
            after,
            jnp.where(has_next, starts[2:3] + ATOMS, far),
            jnp.where(has_prev, starts[1:2] - ATOMS, far),
        )
        side_to = jnp.where(
            after,
            jnp.where(has_next, ends[2:3] + ATOMS, far),
            jnp.where(has_prev, ends[1:2] - ATOMS, far),
        )
        masked = one_lane == MASK_LANE
        low_mask = jnp.where(has_prev, far, -float(MARGIN))
        mask_from = jnp.where(has_next, low_mask, float(ATOMS))
        mask_to = jnp.where(
            has_next, jnp.where(has_prev, far, 0.0), float(ATOMS + MARGIN)
        )
        side_from = jnp.where(masked, mask_from, side_from)
        side_to = jnp.where(masked, mask_to, side_to)

        def onehot(first, count, lo, hi):
            at = (iota((count, TOK), 0) + first).astype(F32)
            return jnp.where((at >= lo) & (at < hi), 1.0, 0.0).astype(BF16)

        rhs[:, CH : CH + TOK] = onehot(-MARGIN, EXT, starts[0:1], ends[0:1])
        for first in (0, ATOMS - 2 * MARGIN + WIN):
            rhs[first : first + KEYS + WIN, CH + TOK :] = onehot(
                first - MARGIN, KEYS + WIN, side_from, side_to
            )
        vals[:, CH:] = jnp.ones((EXT, CH), BF16)
        at = iota((TOK, ATOMS), 1).astype(F32)
        member[...] = jnp.where(
            (at >= starts_column) & (at < ends_column), 1.0, 0.0
        ).astype(BF16)

        weights[0].wait()
        w32 = bias_weights()
        side_moments(w32)

        @pl.loop(0, steps)
        def _(k):
            own_copy(k).wait()

            @pl.loop(0, STEP, unroll=8)
            def _(u):
                i = k * STEP + u
                moments(own_pair[i], i, 0, w32)

        for w in weights[2:]:
            w.wait()
        pl.semaphore_wait(barrier, greetings)

        @pl.when(to_next)
        def _():
            edge_copy(True, r + 1).start()

        @pl.when(to_prev)
        def _():
            edge_copy(False, r - 1).start()

        own_bias = [value.astype(BF16) for value in head_bias(0, TOK)]
        main_side = head_bias(8 * TOK, HALF)
        for h in range(HEADS):
            for k in range(ATOMS // 256):
                first = k * 256
                rows = mm(
                    rhs[MARGIN + first : MARGIN + first + 256, CH : CH + TOK], own_bias[h]
                ).astype(BF16)
                for w in range(256 // WIN):
                    start = (first + w * WIN) * HEADS + h * WIN
                    picked[start : start + WIN, :] = rows[w * WIN : (w + 1) * WIN]

        own_atoms.wait()
        for col in reversed(row_peers):
            atom_copy(col).wait_recv()

        @pl.when(has_prev)
        def _():
            edge_copy(True, r).wait_recv()

        @pl.when(jnp.logical_not(has_prev))
        def _():
            atoms[0:MARGIN, :] = jnp.zeros((MARGIN, CH), BF16)

        @pl.when(has_next)
        def _():
            edge_copy(False, r).wait_recv()

        @pl.when(jnp.logical_not(has_next))
        def _():
            atoms[MARGIN + ATOMS :, :] = jnp.zeros((MARGIN, CH), BF16)

        pieces = [(0, MARGIN, False)]
        pieces += [(MARGIN + 256 * k, 256, True) for k in range(ATOMS // 256)]
        pieces += [(MARGIN + ATOMS, MARGIN, False)]
        for start, count, inside in pieces:
            span = slice(start, start + count)
            norm = layer_norm(atoms[span, :].astype(F32)).astype(BF16)
            projected = mm(norm, wp[...])
            rhs[span, 0:CH] = projected[:, CH : 2 * CH].astype(BF16)
            vals[span, 0:CH] = projected[:, 2 * CH : 3 * CH].astype(BF16)
            if inside:
                first = slice(start - MARGIN, start - MARGIN + count)
                gate[first, :] = 0.5 + 0.5 * jnp.tanh(0.5 * projected[:, 3 * CH :])
                queries[first, :] = (projected[:, 0:CH] * (CH // HEADS) ** -0.5).astype(BF16)

        @pl.when(has_helper)
        def _():
            side_copy().wait_recv()

        @pl.when(jnp.logical_not(has_helper))
        def _():
            side_in[...] = jnp.zeros(side_in.shape, F32)

        low_lanes = iota((HALF, TOK), 1) < SPLIT
        mask_lane = iota((TOK, TOK), 1) == MASK_LANE
        for h in range(HEADS):
            theirs = side_in[h]
            ahead = jnp.where(on_main_next, main_side[h], theirs)
            behind = jnp.where(on_main_next, theirs, main_side[h])
            ahead_rolled = pltpu.roll(ahead, SPLIT, 1)
            behind_rolled = pltpu.roll(behind, SPLIT, 1)
            none = jnp.zeros((HALF, TOK), F32)
            gap = TOK - REACH - HALF
            upper_rows = jnp.concatenate([none, none[:gap], ahead, ahead_rolled], axis=0)
            lower_rows = jnp.concatenate([behind_rolled, behind, none, none[:gap]], axis=0)
            both = jnp.where(iota((TOK, TOK), 1) < SPLIT, upper_rows, lower_rows)
            both = jnp.where(mask_lane, -1e30, both).astype(BF16)
            for k, first in enumerate((0, ATOMS - 2 * WIN)):
                rows = mm(
                    rhs[MARGIN + first : MARGIN + first + 2 * WIN, CH : CH + TOK], both
                ).astype(BF16)
                for w in range(2):
                    start = ((2 * k + w) * HEADS + h) * WIN
                    picked_side[start : start + WIN, :] = rows[w * WIN : (w + 1) * WIN]

        head_of = iota((WIN, CH), 1) // (CH // HEADS)

        def attend(q, bias, keys, extra, values, opened):
            split = [jnp.where(head_of == h, q, jnp.zeros_like(q)) for h in range(HEADS)]
            parts = [jnp.concatenate(split, axis=0), bias]
            if extra is not None:
                parts.append(extra)
            scores = nt(jnp.concatenate(parts, axis=1), keys)
            top = jnp.max(scores, -1, keepdims=True)
            weight = jnp.exp(scores - top).astype(BF16)
            total = mm(weight, values)
            above = total[0:WIN, 0:CH]
            below = total[0:WIN, CH:]
            for h in range(1, HEADS):
                here = head_of == h
                above = jnp.where(here, total[h * WIN : (h + 1) * WIN, 0:CH], above)
                below = jnp.where(here, total[h * WIN : (h + 1) * WIN, CH:], below)
            return (above * opened / below).astype(BF16)

        for n, w in enumerate(EDGES):
            span = slice(w * WIN, (w + 1) * WIN)
            keys = slice(w * WIN, w * WIN + KEYS)
            block = slice(w * WIN * HEADS, (w + 1) * WIN * HEADS)
            gated[span, :] = attend(
                queries[span, :],
                picked[block, :],
                rhs[keys, :],
                picked_side[n * WIN * HEADS : (n + 1) * WIN * HEADS, :],
                vals[keys, :],
                gate[span, :],
            )

        @pl.loop(2, ATOMS // WIN - 2, unroll=ATTEND_UNROLL)
        def _(w):
            start = pl.multiple_of(w * WIN, WIN)
            span = pl.ds(start, WIN)
            keys = pl.ds(start, KEYS)
            block = pl.ds(pl.multiple_of(w * WIN * HEADS, WIN * HEADS), WIN * HEADS)
            gated[span, :] = attend(
                queries[span, :],
                picked[block, :],
                rhs[keys, 0 : CH + TOK],
                None,
                vals[keys, :],
                gate[span, :],
            )

        for k in range(ATOMS // 256):
            span = slice(k * 256, (k + 1) * 256)
            ext = slice(MARGIN + k * 256, MARGIN + (k + 1) * 256)
            resid[span, :] = (atoms[ext, :].astype(F32) + mm(gated[span, :], wo[...])).astype(BF16)
        for p in range(7):
            resid_send(p).start()
        for k in range(ATOMS // 256):
            span = slice(k * 256, (k + 1) * 256)
            out = transition(resid[span, :])
            emitted[span, :] = jnp.maximum(mm(out, wk[...]), 0.0).astype(BF16)
        totals = mm(member[...], emitted[...])
        single = (totals / counts_column).astype(BF16)
        col_out[pl.ds(pl.multiple_of(odd * TOK, TOK), TOK), :] = mm(single, wc[...]).astype(BF16)
        for p in range(7):
            col_send(p).start()
        single_out[...] = single
        for p in range(7):
            single_send(p).start()
        resid_in[...] = resid[pl.ds(pl.multiple_of(c * OWN, OWN), OWN), :]

    @pl.when(not_main)
    def _():
        for w in receiver_weights:
            w.wait()
        resid_send(0).wait_recv()

    atom_out[...] = transition(resid_in[...])

    @pl.when(fed_by_main)
    def _():
        col_send(0).wait_recv()

    col_forward().start()

    @pl.when(not_main)
    def _():
        single_send(0).wait_recv()

    row_out[...] = mm(single_out[...], wr[...])
    col_forward().wait_recv()
    col_forward().wait_send()

    @pl.when(is_main)
    def _():
        for p in range(7):
            resid_send(p).wait_send()
            col_send(p).wait_send()
            single_send(p).wait_send()

    @pl.when(not_main)
    def _():
        atom_copy(c).wait_send()

    @pl.when(to_next)
    def _():
        edge_copy(True, r + 1).wait_send()

    @pl.when(to_prev)
    def _():
        edge_copy(False, r - 1).wait_send()


def update_kernel(pair, row, col, atom, single, new_pair, atom_out, single_out):
    @pl.when(pl.program_id(0) == 0)
    def _():
        atom_out[...] = atom[...]
        single_out[...] = single[...]

    column = col[...]
    for i in range(pair.shape[0]):
        term = jnp.broadcast_to(row[i : i + 1, :], (16, CH)).astype(BF16)
        term = jnp.concatenate([term] * (column.shape[0] // 16), axis=0)
        new_pair[i] = pair[i] + (column + term)


def shards(
    pair, counts, atom_single, w_bias, w_project, w_out, w_trans_in, w_trans_out, w_token, w_row, w_col
):
    any_ = pl.BlockSpec(memory_space=pl.ANY)
    vmem = pltpu.VMEM
    in_hbm = lambda a: pltpu.with_memory_space_constraint(a, pltpu.HBM)
    weights = (w_bias.T, w_project, w_out, w_trans_in, w_trans_out, w_token, w_row, w_col)
    in_vmem = pl.BlockSpec(memory_space=vmem)
    atom, single, row, col = pl.pallas_call(
        exchange_kernel,
        out_shape=(
            jax.ShapeDtypeStruct((OWN, CH), BF16),
            jax.ShapeDtypeStruct((TOK, 3 * CH), BF16),
            jax.ShapeDtypeStruct((TOK, CH), F32),
            jax.ShapeDtypeStruct((2 * TOK, CH), BF16),
        ),
        in_specs=[any_] * (3 + len(weights)),
        out_specs=(in_vmem,) * 4,
        scratch_shapes=[
            vmem((TOK, TOK, CH), BF16),
            vmem((HALF, TOK, CH), BF16),
            vmem(counts.shape, jnp.int32),
            *[vmem(w.shape, w.dtype) for w in weights],
            vmem((8 * (TOK + HALF), TOK), F32),
            vmem((8 * (TOK + HALF), TOK), F32),
            vmem((HEADS, HALF, TOK), F32),
            vmem((HEADS, HALF, TOK), F32),
            vmem((EXT, CH), BF16),
            vmem((ATOMS, CH), BF16),
            vmem((ATOMS * HEADS, TOK), BF16),
            vmem((len(EDGES) * WIN * HEADS, TOK), BF16),
            vmem((EXT, CH + 2 * TOK), BF16),
            vmem((EXT, 2 * CH), BF16),
            vmem((ATOMS, CH), F32),
            vmem((ATOMS, CH), BF16),
            vmem((ATOMS, CH), BF16),
            vmem((OWN, CH), BF16),
            vmem((ATOMS, 3 * CH), BF16),
            vmem((TOK, ATOMS), BF16),
            pltpu.SemaphoreType.DMA((TOK // STEP,)),
            pltpu.SemaphoreType.DMA((2,)),
            pltpu.SemaphoreType.DMA((1 + len(weights),)),
            pltpu.SemaphoreType.DMA((1,)),
            pltpu.SemaphoreType.DMA((29,)),
            pltpu.SemaphoreType.DMA((N_COL + 7,)),
        ],
        compiler_params=pltpu.CompilerParams(
            collective_id=0, has_side_effects=True, vmem_limit_bytes=40 * 2**20
        ),
    )(*[in_hbm(a) for a in (pair, atom_single, counts, *weights)])
    rows = 16
    whole = lambda a: pl.BlockSpec(a.shape, lambda i: (0,) * a.ndim)
    block = pl.BlockSpec((rows,) + pair.shape[1:], lambda i: (i, 0, 0))
    new_pair, atom_out, token_single = pl.pallas_call(
        update_kernel,
        grid=(pair.shape[0] // rows,),
        out_shape=(
            jax.ShapeDtypeStruct(pair.shape, BF16),
            jax.ShapeDtypeStruct(atom.shape, BF16),
            jax.ShapeDtypeStruct(single.shape, BF16),
        ),
        in_specs=[
            block,
            pl.BlockSpec((rows, CH), lambda i: (i, 0)),
            whole(col),
            whole(atom),
            whole(single),
        ],
        out_specs=(block, whole(atom), whole(single)),
        compiler_params=pltpu.CompilerParams(vmem_limit_bytes=16 * 2**20),
    )(pair, row, col, atom, single)
    return atom_out, token_single, new_pair


def solution(mesh):
    return jax.shard_map(
        shards,
        mesh=mesh,
        in_specs=(P("row", "col", None), P(), P(("row", "col"), None)) + (P(),) * 8,
        out_specs=(P(("row", "col"), None), P("row", None), P("row", "col", None)),
        check_vma=False,
    )
```

time: 75.9 us -> 39.3 us (0.52)
  the two profiles are of different devices: /device:TPU:12 before, /device:TPU:4 now
where the time goes in v2:
time: 39.3 us; the launch traced here: 39.2 us
  Pallas kernels  38.5 us (98%)
  between operations  0.66 us (2%)
    pallas_call x1, Pallas kernels, shards(): pl.pallas_call(exchange_kernel, out_shape=(jax.ShapeDtypeStruct((OWN, CH)...  33.5 us
    pallas_call x1, Pallas kernels, shards(): pl.pallas_call(update_kernel, grid=(pair.shape[0] // rows,), out_shape=(j...  5 us

profile of v2, /device:TPU:4, one launch (start us, length us, event | category | flops | bytes accessed | tf_op | source)
XLA Modules:
  0.0 39.2 jit_solution(15208249909602045889)
XLA Ops:
  0.6 0.0 copy-start
  0.6 33.5 %shard_map.130 = (bf16[128,128]{1,0:T(8,128)(2,1)S(1)}, bf16[128,384]{1,0:T(8,128)(2,1)S(1)}, f32[128,128]{1,0:T(8,128)S(1)}, bf16[256,128]{1,0:T(8,128)(2,1)S(1)}) custom-call(bf16[128,256,128]{2,1,0:T(8,128)(2,1)} %pair.1, bf16[128,128]{1,0:T(8,128)(2,1)} %atom_hbm.1, s32[16,128]{1,0:T(8,128)} %counts_hbm.1, f32[4,128]{1,0:T(4,128)} %bitcast.1, ...), custom_call_target="tpu_custom_call" | custom-call | tf_op jit(solution)/shard_map/pallas_call | solution.py:669
  34.2 0.0 copy-done
  34.2 5.0 %shard_map.131 = (bf16[128,256,128]{2,1,0:T(8,128)(2,1)}, bf16[128,128]{1,0:T(8,128)(2,1)}, bf16[128,384]{1,0:T(8,128)(2,1)}) custom-call(bf16[128,256,128]{2,1,0:T(8,128)(2,1)S(1)} %copy-done, f32[128,128]{1,0:T(8,128)S(1)} %get-tuple-element.10.row, bf16[256,128]{1,0:T(8,128)(2,1)S(1)} %get-tuple-element.11.col, ...), custom_call_target="tpu_custom_call" | custom-call | tf_op jit(solution)/shard_map/pallas_call | solution.py:714
Async XLA Ops:
  0.6 33.5 %copy-start = (bf16[128,256,128]{2,1,0:T(8,128)(2,1)S(1)}, bf16[128,256,128]{2,1,0:T(8,128)(2,1)}, u32[]{:S(2)}) copy-start(bf16[128,256,128]{2,1,0:T(8,128)(2,1)} %pair.1) | copy-start | bytes 25165828

commit v3 on v2

--- a/solution.py
+++ b/solution.py
@@ -21,11 +21,14 @@
 EXT = ATOMS + 2 * MARGIN
 OWN = ATOMS // N_COL
 STEP = 16
+BLOCK = 8
+UPDATE_VMEM = 20
 REACH = 80
 HALF = REACH // 2
+EARLY = 4
 EDGES = (0, 1, 30, 31)
 MASK_LANE = 56
-ATTEND_UNROLL = 14
+ATTEND_UNROLL = 28
 SPLIT = 64
 
 
@@ -89,6 +92,7 @@
     gated,
     resid,
     resid_in,
+    final,
     emitted,
     member,
     own_sem,
@@ -110,8 +114,9 @@
     z, x_hi = c // 2, lax.rem(c, 2)
     y, x_lo = r // 4, lax.rem(r // 2, 2)
     sibling = r + 1 - 2 * odd
+    partner = c + 1 - 2 * x_hi
+    home_side = x_hi == x_lo
     col_main = 2 * c + odd
-    fed_by_main = r != col_main
     row_peers = [
         (lax.rem(z + dz, 4) * 2 + (1 - x_hi if dx else x_hi))
         for dz, dx in ((2, 1), (1, 1), (3, 1), (2, 0), (0, 1), (1, 0), (3, 0))
@@ -166,6 +171,8 @@
     to_next = (c == N_COL - 1) & has_next
     to_prev = (c == 0) & has_prev
 
+    relays = not_main & home_side
+
     @pl.when(is_main)
     def _():
         for col in row_peers:
@@ -179,35 +186,25 @@
         def _():
             hello(r + 1, 0)
 
-        for row in col_peers:
-            hello(row, c)
-
     @pl.when(not_main)
     def _():
         hello(r, home)
-
-    @pl.when(fed_by_main)
-    def _():
         hello(col_main, c)
 
     hello(sibling, c)
 
-    @pl.when(to_next)
-    def _():
-        hello(r + 1, (r + 1) // 2)
-
-    @pl.when(to_prev)
-    def _():
-        hello(r - 1, (r - 1) // 2)
+    @pl.when(jnp.logical_not(home_side) & (partner != home))
+    def _():
+        hello(r, partner)
 
     def one(flag):
         return jnp.where(flag, 1, 0)
 
     greetings = (
         1
-        + one(is_main) * (2 * 7 + one(has_prev) + one(has_next))
+        + one(is_main) * 2 * 7
         + one(not_main)
-        + one(fed_by_main)
+        + one(relays)
         + one(to_next)
         + one(to_prev)
     )
@@ -272,19 +269,6 @@
     @pl.when(is_main)
     def _():
         own_atoms.start()
-
-    @pl.when(not_main)
-    def _():
-        pl.semaphore_wait(barrier, greetings)
-        atom_copy(c).start()
-
-    @pl.when(to_next & not_main)
-    def _():
-        edge_copy(True, r + 1).start()
-
-    @pl.when(to_prev & not_main)
-    def _():
-        edge_copy(False, r - 1).start()
 
     lane = iota((8, TOK), 1)
     sub = iota((8, TOK), 0)
@@ -350,6 +334,22 @@
         side_moments(bias_weights())
         for h, value in enumerate(head_bias(8 * TOK, HALF)):
             side[h] = value
+
+    @pl.when(not_main)
+    def _():
+        pl.semaphore_wait(barrier, greetings)
+        atom_copy(c).start()
+
+    @pl.when(to_next & not_main)
+    def _():
+        edge_copy(True, r + 1).start()
+
+    @pl.when(to_prev & not_main)
+    def _():
+        edge_copy(False, r - 1).start()
+
+    @pl.when(is_helper)
+    def _():
         side_copy().start()
         side_copy().wait_send()
 
@@ -369,16 +369,18 @@
         col = row_peers[p]
         return send(resid.at[pl.ds(col * OWN, OWN)], resid_in, 4 + p, base, r, col)
 
-    def single_send(p):
-        return send(single_out, single_out, 12 + p, base + 1, r, row_peers[p])
+    def single_send(p, k):
+        piece = single_out.at[:, pl.ds(k * CH, CH)]
+        col = (row_peers[3], row_peers[5], row_peers[6], partner)[p]
+        return send(piece, piece, 12 + 4 * k + p, base + (1, 4, 5)[k], r, col)
 
     own_half = col_out.at[pl.ds(pl.multiple_of(odd * TOK, TOK), TOK)]
 
     def col_send(p):
-        return send(own_half, own_half, 20 + p, base + 2, col_peers[p], c)
+        return send(own_half, own_half, 24 + p, base + 2, col_peers[p], c)
 
     def col_forward():
-        return send(own_half, own_half, 28, base + 3, sibling, c)
+        return send(own_half, own_half, 31, base + 3, sibling, c)
 
     @pl.when(is_main)
     def _():
@@ -472,39 +474,26 @@
                     start = (first + w * WIN) * HEADS + h * WIN
                     picked[start : start + WIN, :] = rows[w * WIN : (w + 1) * WIN]
 
-        own_atoms.wait()
-        for col in reversed(row_peers):
-            atom_copy(col).wait_recv()
-
-        @pl.when(has_prev)
-        def _():
-            edge_copy(True, r).wait_recv()
-
-        @pl.when(jnp.logical_not(has_prev))
-        def _():
-            atoms[0:MARGIN, :] = jnp.zeros((MARGIN, CH), BF16)
-
-        @pl.when(has_next)
-        def _():
-            edge_copy(False, r).wait_recv()
-
-        @pl.when(jnp.logical_not(has_next))
-        def _():
-            atoms[MARGIN + ATOMS :, :] = jnp.zeros((MARGIN, CH), BF16)
-
-        pieces = [(0, MARGIN, False)]
-        pieces += [(MARGIN + 256 * k, 256, True) for k in range(ATOMS // 256)]
-        pieces += [(MARGIN + ATOMS, MARGIN, False)]
-        for start, count, inside in pieces:
-            span = slice(start, start + count)
+        def keys_values(start, count):
+            span = pl.ds(start, count)
             norm = layer_norm(atoms[span, :].astype(F32)).astype(BF16)
             projected = mm(norm, wp[...])
             rhs[span, 0:CH] = projected[:, CH : 2 * CH].astype(BF16)
             vals[span, 0:CH] = projected[:, 2 * CH : 3 * CH].astype(BF16)
-            if inside:
-                first = slice(start - MARGIN, start - MARGIN + count)
-                gate[first, :] = 0.5 + 0.5 * jnp.tanh(0.5 * projected[:, 3 * CH :])
-                queries[first, :] = (projected[:, 0:CH] * (CH // HEADS) ** -0.5).astype(BF16)
+            return projected
+
+        def project(col):
+            projected = keys_values(pl.multiple_of(MARGIN + col * OWN, 16), OWN)
+            span = pl.ds(pl.multiple_of(col * OWN, OWN), OWN)
+            gate[span, :] = 0.5 + 0.5 * jnp.tanh(0.5 * projected[:, 3 * CH :])
+            queries[span, :] = (projected[:, 0:CH] * (CH // HEADS) ** -0.5).astype(BF16)
+
+        own_atoms.wait()
+        near_first = row_peers[::-1]
+        for col in near_first[:EARLY]:
+            atom_copy(col).wait_recv()
+        for col in [c] + near_first[:EARLY]:
+            project(col)
 
         @pl.when(has_helper)
         def _():
@@ -536,6 +525,30 @@
                     start = ((2 * k + w) * HEADS + h) * WIN
                     picked_side[start : start + WIN, :] = rows[w * WIN : (w + 1) * WIN]
 
+        for col in near_first[EARLY:]:
+            atom_copy(col).wait_recv()
+
+        @pl.when(has_prev)
+        def _():
+            edge_copy(True, r).wait_recv()
+
+        @pl.when(jnp.logical_not(has_prev))
+        def _():
+            atoms[0:MARGIN, :] = jnp.zeros((MARGIN, CH), BF16)
+
+        @pl.when(has_next)
+        def _():
+            edge_copy(False, r).wait_recv()
+
+        @pl.when(jnp.logical_not(has_next))
+        def _():
+            atoms[MARGIN + ATOMS :, :] = jnp.zeros((MARGIN, CH), BF16)
+
+        for col in near_first[EARLY:]:
+            project(col)
+        keys_values(0, MARGIN)
+        keys_values(MARGIN + ATOMS, MARGIN)
+
         head_of = iota((WIN, CH), 1) // (CH // HEADS)
 
         def attend(q, bias, keys, extra, values, opened):
@@ -591,16 +604,22 @@
             resid_send(p).start()
         for k in range(ATOMS // 256):
             span = slice(k * 256, (k + 1) * 256)
-            out = transition(resid[span, :])
-            emitted[span, :] = jnp.maximum(mm(out, wk[...]), 0.0).astype(BF16)
-        totals = mm(member[...], emitted[...])
-        single = (totals / counts_column).astype(BF16)
-        col_out[pl.ds(pl.multiple_of(odd * TOK, TOK), TOK), :] = mm(single, wc[...]).astype(BF16)
+            final[span, :] = transition(resid[span, :])
+        terms = jnp.zeros((TOK, CH), F32)
+        for q in range(3):
+            part = slice(q * CH, (q + 1) * CH)
+            for k in range(ATOMS // 256):
+                span = slice(k * 256, (k + 1) * 256)
+                emitted[span, part] = jnp.maximum(mm(final[span, :], wk[:, part]), 0.0).astype(BF16)
+            totals = mm(member[...], emitted[:, part])
+            single = (totals / counts_column).astype(BF16)
+            single_out[:, part] = single
+            for p in range(4):
+                single_send(p, q).start()
+            terms = terms + mm(single, wc[part, :])
+        col_out[pl.ds(pl.multiple_of(odd * TOK, TOK), TOK), :] = terms.astype(BF16)
         for p in range(7):
             col_send(p).start()
-        single_out[...] = single
-        for p in range(7):
-            single_send(p).start()
         resid_in[...] = resid[pl.ds(pl.multiple_of(c * OWN, OWN), OWN), :]
 
     @pl.when(not_main)
@@ -611,15 +630,22 @@
 
     atom_out[...] = transition(resid_in[...])
 
-    @pl.when(fed_by_main)
+    @pl.when(relays)
+    def _():
+        for k in range(3):
+            single_send(0, k).wait_recv()
+            single_send(3, k).start()
+
+    @pl.when(not_main)
     def _():
         col_send(0).wait_recv()
 
     col_forward().start()
 
-    @pl.when(not_main)
-    def _():
-        single_send(0).wait_recv()
+    @pl.when(jnp.logical_not(home_side))
+    def _():
+        for k in range(3):
+            single_send(0, k).wait_recv()
 
     row_out[...] = mm(single_out[...], wr[...])
     col_forward().wait_recv()
@@ -630,7 +656,14 @@
         for p in range(7):
             resid_send(p).wait_send()
             col_send(p).wait_send()
-            single_send(p).wait_send()
+        for k in range(3):
+            for p in range(4):
+                single_send(p, k).wait_send()
+
+    @pl.when(relays)
+    def _():
+        for k in range(3):
+            single_send(3, k).wait_send()
 
     @pl.when(not_main)
     def _():
@@ -645,17 +678,34 @@
         edge_copy(False, r - 1).wait_send()
 
 
-def update_kernel(pair, row, col, atom, single, new_pair, atom_out, single_out):
-    @pl.when(pl.program_id(0) == 0)
-    def _():
-        atom_out[...] = atom[...]
-        single_out[...] = single[...]
-
+def update_kernel(pair, row, col, atom, single, new_pair, atom_out, single_out, result, sem):
+    small = [
+        pltpu.make_async_copy(atom, atom_out, sem.at[0]),
+        pltpu.make_async_copy(single, single_out, sem.at[1]),
+    ]
+    for copy in small:
+        copy.start()
+    width = col.shape[0]
     column = col[...]
-    for i in range(pair.shape[0]):
-        term = jnp.broadcast_to(row[i : i + 1, :], (16, CH)).astype(BF16)
-        term = jnp.concatenate([term] * (column.shape[0] // 16), axis=0)
-        new_pair[i] = pair[i] + (column + term)
+
+    def out_copy(k):
+        rows = pl.ds(k * BLOCK, BLOCK)
+        return pltpu.make_async_copy(result.at[rows], new_pair.at[rows], sem.at[2 + k])
+
+    @pl.loop(0, TOK // BLOCK)
+    def _(k):
+        terms = row[pl.ds(pl.multiple_of(k * BLOCK, BLOCK), BLOCK), :]
+        for u in range(BLOCK):
+            term = jnp.broadcast_to(terms[u : u + 1], (16, CH)).astype(BF16)
+            term = jnp.concatenate([term] * (width // 16), axis=0)
+            i = k * BLOCK + u
+            result[i] = pair[i] + (column + term)
+        out_copy(k).start()
+
+    for copy in small:
+        copy.wait()
+    for k in range(TOK // BLOCK):
+        out_copy(k).wait()
 
 
 def shards(
@@ -695,40 +745,35 @@
             vmem((ATOMS, CH), BF16),
             vmem((ATOMS, CH), BF16),
             vmem((OWN, CH), BF16),
+            vmem((ATOMS, CH), BF16),
             vmem((ATOMS, 3 * CH), BF16),
             vmem((TOK, ATOMS), BF16),
             pltpu.SemaphoreType.DMA((TOK // STEP,)),
             pltpu.SemaphoreType.DMA((2,)),
             pltpu.SemaphoreType.DMA((1 + len(weights),)),
             pltpu.SemaphoreType.DMA((1,)),
-            pltpu.SemaphoreType.DMA((29,)),
-            pltpu.SemaphoreType.DMA((N_COL + 7,)),
+            pltpu.SemaphoreType.DMA((32,)),
+            pltpu.SemaphoreType.DMA((N_COL + 9,)),
         ],
         compiler_params=pltpu.CompilerParams(
             collective_id=0, has_side_effects=True, vmem_limit_bytes=40 * 2**20
         ),
     )(*[in_hbm(a) for a in (pair, atom_single, counts, *weights)])
-    rows = 16
-    whole = lambda a: pl.BlockSpec(a.shape, lambda i: (0,) * a.ndim)
-    block = pl.BlockSpec((rows,) + pair.shape[1:], lambda i: (i, 0, 0))
     new_pair, atom_out, token_single = pl.pallas_call(
         update_kernel,
-        grid=(pair.shape[0] // rows,),
         out_shape=(
             jax.ShapeDtypeStruct(pair.shape, BF16),
             jax.ShapeDtypeStruct(atom.shape, BF16),
             jax.ShapeDtypeStruct(single.shape, BF16),
         ),
-        in_specs=[
-            block,
-            pl.BlockSpec((rows, CH), lambda i: (i, 0)),
-            whole(col),
-            whole(atom),
-            whole(single),
+        in_specs=[in_vmem] * 5,
+        out_specs=(any_,) * 3,
+        scratch_shapes=[
+            vmem(pair.shape, BF16),
+            pltpu.SemaphoreType.DMA((2 + TOK // BLOCK,)),
         ],
-        out_specs=(block, whole(atom), whole(single)),
-        compiler_params=pltpu.CompilerParams(vmem_limit_bytes=16 * 2**20),
-    )(pair, row, col, atom, single)
+        compiler_params=pltpu.CompilerParams(vmem_limit_bytes=UPDATE_VMEM * 2**20),
+    )(pltpu.with_memory_space_constraint(pair, pltpu.VMEM), row, col, atom, single)
     return atom_out, token_single, new_pair
 
 

time: 39.3 us -> 32.7 us (0.83)
  the two profiles are of different devices: /device:TPU:4 before, /device:TPU:18 now
where the time goes in v3:
time: 32.7 us; the launch traced here: 32.6 us
  Pallas kernels  31.9 us (98%)
  between operations  0.66 us (2%)
    pallas_call x1, Pallas kernels, shards(): pl.pallas_call(exchange_kernel, out_shape=(jax.ShapeDtypeStruct((OWN, CH)...  28.4 us
    pallas_call x1, Pallas kernels, shards(): pl.pallas_call(update_kernel, out_shape=(jax.ShapeDtypeStruct(pair.shape,...  3.53 us

profile of v3, /device:TPU:18, one launch (start us, length us, event | category | flops | bytes accessed | tf_op | source)
XLA Modules:
  0.0 32.6 jit_solution(17324169520402714212)
XLA Ops:
  0.6 0.0 copy-start
  0.6 28.4 %shard_map.130 = (bf16[128,128]{1,0:T(8,128)(2,1)S(1)}, bf16[128,384]{1,0:T(8,128)(2,1)S(1)}, f32[128,128]{1,0:T(8,128)S(1)}, bf16[256,128]{1,0:T(8,128)(2,1)S(1)}) custom-call(bf16[128,256,128]{2,1,0:T(8,128)(2,1)} %pair.1, bf16[128,128]{1,0:T(8,128)(2,1)} %atom_hbm.1, s32[16,128]{1,0:T(8,128)} %counts_hbm.1, f32[4,128]{1,0:T(4,128)} %bitcast.1, ...), custom_call_target="tpu_custom_call" | custom-call | tf_op jit(solution)/shard_map/pallas_call | solution.py:719
  29.0 0.0 copy-done
  29.0 3.5 %shard_map.131 = (bf16[128,256,128]{2,1,0:T(8,128)(2,1)}, bf16[128,128]{1,0:T(8,128)(2,1)}, bf16[128,384]{1,0:T(8,128)(2,1)}) custom-call(bf16[128,256,128]{2,1,0:T(8,128)(2,1)S(1)} %copy-done, f32[128,128]{1,0:T(8,128)S(1)} %get-tuple-element.10.row, bf16[256,128]{1,0:T(8,128)(2,1)S(1)} %get-tuple-element.11.col, ...), custom_call_target="tpu_custom_call" | custom-call | tf_op jit(solution)/shard_map/pallas_call | solution.py:762
Async XLA Ops:
  0.6 28.4 %copy-start = (bf16[128,256,128]{2,1,0:T(8,128)(2,1)S(1)}, bf16[128,256,128]{2,1,0:T(8,128)(2,1)}, u32[]{:S(2)}) copy-start(bf16[128,256,128]{2,1,0:T(8,128)(2,1)} %pair.1) | copy-start | bytes 25165828

commit v4 on v3

--- a/solution.py
+++ b/solution.py
@@ -29,6 +29,9 @@
 EDGES = (0, 1, 30, 31)
 MASK_LANE = 56
 ATTEND_UNROLL = 28
+OWN_UNROLL = 64
+SIDE_UNROLL = 40
+PART = 256
 SPLIT = 64
 
 
@@ -92,6 +95,7 @@
     gated,
     resid,
     resid_in,
+    mine_in,
     final,
     emitted,
     member,
@@ -163,6 +167,11 @@
     receiver_weights = [weights[4], weights[5], weights[7]]
     steps = TOK // STEP
 
+    own_atoms = pltpu.make_async_copy(
+        atom_hbm, atoms.at[pl.ds(MARGIN + c * OWN, OWN)], local_sem.at[0]
+    )
+    mine = pltpu.make_async_copy(atom_hbm, mine_in, local_sem.at[1])
+    mine.start()
     barrier = pltpu.get_barrier_semaphore()
 
     def hello(row, col):
@@ -171,7 +180,11 @@
     to_next = (c == N_COL - 1) & has_next
     to_prev = (c == 0) & has_prev
 
-    relays = not_main & home_side
+    across = jnp.logical_not(home_side)
+    ahead_of_home = lax.rem(z - y + 4, 4)
+    relays = not_main & ((home_side & (ahead_of_home != 2)) | (across & (ahead_of_home == 0)))
+    passes_atoms = not_main & home_side
+    feeder = jnp.where(home_side, lax.rem(z + 3, 4), lax.rem(z + 2, 4)) * 2 + x_hi
 
     @pl.when(is_main)
     def _():
@@ -193,9 +206,13 @@
 
     hello(sibling, c)
 
-    @pl.when(jnp.logical_not(home_side) & (partner != home))
+    @pl.when(across & (ahead_of_home != 0))
     def _():
         hello(r, partner)
+
+    @pl.when(ahead_of_home == 2)
+    def _():
+        hello(r, feeder)
 
     def one(flag):
         return jnp.where(flag, 1, 0)
@@ -204,7 +221,9 @@
         1
         + one(is_main) * 2 * 7
         + one(not_main)
-        + one(relays)
+        + one(passes_atoms)
+        + one(ahead_of_home == 1) * one(home_side)
+        + one(ahead_of_home == 0) * one(across)
         + one(to_next)
         + one(to_prev)
     )
@@ -212,6 +231,7 @@
     @pl.when(is_main)
     def _():
         weights[1].start()
+        own_atoms.start()
         weights[0].start()
         for k in range(2):
             side_pair_copy(k).start()
@@ -233,7 +253,7 @@
 
     def atom_copy(col):
         return pltpu.make_async_remote_copy(
-            src_ref=atom_hbm,
+            src_ref=mine_in,
             dst_ref=atoms.at[pl.ds(MARGIN + col * OWN, OWN)],
             send_sem=send_sem.at[0],
             recv_sem=recv_sem.at[col],
@@ -244,7 +264,7 @@
     def edge_copy(forward, row):
         start = OWN - MARGIN if forward else 0
         return pltpu.make_async_remote_copy(
-            src_ref=atom_hbm.at[pl.ds(start, MARGIN)],
+            src_ref=mine_in.at[pl.ds(start, MARGIN)],
             dst_ref=atoms.at[pl.ds(0 if forward else MARGIN + ATOMS, MARGIN)],
             send_sem=send_sem.at[1 if forward else 2],
             recv_sem=recv_sem.at[N_COL + (0 if forward else 1)],
@@ -262,13 +282,6 @@
             device_id_type=MESH,
         )
 
-    own_atoms = pltpu.make_async_copy(
-        atom_hbm, atoms.at[pl.ds(MARGIN + c * OWN, OWN)], local_sem.at[0]
-    )
-
-    @pl.when(is_main)
-    def _():
-        own_atoms.start()
 
     lane = iota((8, TOK), 1)
     sub = iota((8, TOK), 0)
@@ -301,7 +314,7 @@
         for k in range(2):
             side_pair_copy(k).wait()
 
-        @pl.loop(0, HALF, unroll=8)
+        @pl.loop(0, HALF, unroll=SIDE_UNROLL)
         def _(i):
             moments(side_pair[i], i, 8 * TOK, w32)
 
@@ -337,6 +350,7 @@
 
     @pl.when(not_main)
     def _():
+        mine.wait()
         pl.semaphore_wait(barrier, greetings)
         atom_copy(c).start()
 
@@ -366,13 +380,39 @@
     base = N_COL + 3
 
     def resid_send(p):
-        col = row_peers[p]
-        return send(resid.at[pl.ds(col * OWN, OWN)], resid_in, 4 + p, base, r, col)
+        col = (partner, row_peers[5], row_peers[6], row_peers[3])[p]
+        count = OWN if p == 0 else 2 * OWN
+        first = col if p == 0 else col // 2 * 2
+        return send(
+            resid.at[pl.ds(pl.multiple_of(first * OWN, OWN), count)],
+            resid_in.at[pl.ds(0, count)],
+            4 + p,
+            base,
+            r,
+            col,
+        )
+
+    def atom_pass():
+        return send(
+            resid_in.at[pl.ds(pl.multiple_of((1 - x_hi) * OWN, OWN), OWN)],
+            atom_out,
+            8,
+            base + 6,
+            r,
+            partner,
+        )
 
     def single_send(p, k):
-        piece = single_out.at[:, pl.ds(k * CH, CH)]
-        col = (row_peers[3], row_peers[5], row_peers[6], partner)[p]
+        piece = single_out.at[k]
+        col = (row_peers[5], row_peers[6], partner, row_peers[3])[p]
         return send(piece, piece, 12 + 4 * k + p, base + (1, 4, 5)[k], r, col)
+
+    tree = (
+        (is_main, (0, 1, 2)),
+        (home_side & (ahead_of_home == 1), (0, 2)),
+        (home_side & (ahead_of_home == 3), (2,)),
+        (across & (ahead_of_home == 0), (3,)),
+    )
 
     own_half = col_out.at[pl.ds(pl.multiple_of(odd * TOK, TOK), TOK)]
 
@@ -441,17 +481,17 @@
         w32 = bias_weights()
         side_moments(w32)
 
-        @pl.loop(0, steps)
+        @pl.loop(0, TOK // OWN_UNROLL)
         def _(k):
-            own_copy(k).wait()
-
-            @pl.loop(0, STEP, unroll=8)
-            def _(u):
-                i = k * STEP + u
+            for u in range(OWN_UNROLL // STEP):
+                own_copy(k * (OWN_UNROLL // STEP) + u).wait()
+            for u in range(OWN_UNROLL):
+                i = k * OWN_UNROLL + u
                 moments(own_pair[i], i, 0, w32)
 
         for w in weights[2:]:
             w.wait()
+        mine.wait()
         pl.semaphore_wait(barrier, greetings)
 
         @pl.when(to_next)
@@ -462,6 +502,10 @@
         def _():
             edge_copy(False, r - 1).start()
 
+        own_atoms.wait()
+        near_first = row_peers[::-1]
+        for col in near_first[:EARLY]:
+            atom_copy(col).wait_recv()
         own_bias = [value.astype(BF16) for value in head_bias(0, TOK)]
         main_side = head_bias(8 * TOK, HALF)
         for h in range(HEADS):
@@ -488,10 +532,6 @@
             gate[span, :] = 0.5 + 0.5 * jnp.tanh(0.5 * projected[:, 3 * CH :])
             queries[span, :] = (projected[:, 0:CH] * (CH // HEADS) ** -0.5).astype(BF16)
 
-        own_atoms.wait()
-        near_first = row_peers[::-1]
-        for col in near_first[:EARLY]:
-            atom_copy(col).wait_recv()
         for col in [c] + near_first[:EARLY]:
             project(col)
 
@@ -600,10 +640,10 @@
             span = slice(k * 256, (k + 1) * 256)
             ext = slice(MARGIN + k * 256, MARGIN + (k + 1) * 256)
             resid[span, :] = (atoms[ext, :].astype(F32) + mm(gated[span, :], wo[...])).astype(BF16)
-        for p in range(7):
+        for p in range(4):
             resid_send(p).start()
-        for k in range(ATOMS // 256):
-            span = slice(k * 256, (k + 1) * 256)
+        for k in range(ATOMS // PART):
+            span = slice(k * PART, (k + 1) * PART)
             final[span, :] = transition(resid[span, :])
         terms = jnp.zeros((TOK, CH), F32)
         for q in range(3):
@@ -613,57 +653,81 @@
                 emitted[span, part] = jnp.maximum(mm(final[span, :], wk[:, part]), 0.0).astype(BF16)
             totals = mm(member[...], emitted[:, part])
             single = (totals / counts_column).astype(BF16)
-            single_out[:, part] = single
-            for p in range(4):
+            single_out[q] = single
+            for p in tree[0][1]:
                 single_send(p, q).start()
             terms = terms + mm(single, wc[part, :])
         col_out[pl.ds(pl.multiple_of(odd * TOK, TOK), TOK), :] = terms.astype(BF16)
         for p in range(7):
             col_send(p).start()
-        resid_in[...] = resid[pl.ds(pl.multiple_of(c * OWN, OWN), OWN), :]
+        resid_in[0:OWN, :] = resid[pl.ds(pl.multiple_of(c * OWN, OWN), OWN), :]
 
     @pl.when(not_main)
     def _():
         for w in receiver_weights:
             w.wait()
+
+    @pl.when(passes_atoms)
+    def _():
+        resid_send(1).wait_recv()
+        resid_in[...] = transition(resid_in[...])
+        atom_pass().start()
+        atom_out[...] = resid_in[pl.ds(pl.multiple_of(x_hi * OWN, OWN), OWN), :]
+
+    @pl.when(across & (ahead_of_home == 0))
+    def _():
         resid_send(0).wait_recv()
 
-    atom_out[...] = transition(resid_in[...])
-
-    @pl.when(relays)
+    @pl.when(ahead_of_home == 0)
+    def _():
+        atom_out[...] = transition(resid_in[0:OWN, :])
+
+    for role, copies in tree[1:]:
+
+        @pl.when(role)
+        def _():
+            for k in range(3):
+                single_send(0, k).wait_recv()
+                for p in copies:
+                    single_send(p, k).start()
+
+    @pl.when(not_main)
+    def _():
+        col_send(0).wait_recv()
+
+    col_forward().start()
+
+    @pl.when(not_main & jnp.logical_not(relays))
     def _():
         for k in range(3):
             single_send(0, k).wait_recv()
-            single_send(3, k).start()
-
-    @pl.when(not_main)
-    def _():
-        col_send(0).wait_recv()
-
-    col_forward().start()
-
-    @pl.when(jnp.logical_not(home_side))
-    def _():
-        for k in range(3):
-            single_send(0, k).wait_recv()
-
-    row_out[...] = mm(single_out[...], wr[...])
+
+    row_out[...] = sum(mm(single_out[q], wr[q * CH : (q + 1) * CH, :]) for q in range(3))
     col_forward().wait_recv()
     col_forward().wait_send()
 
+    @pl.when(passes_atoms)
+    def _():
+        atom_pass().wait_send()
+
+    @pl.when(across & (ahead_of_home != 0))
+    def _():
+        atom_pass().wait_recv()
+
     @pl.when(is_main)
     def _():
+        for p in range(4):
+            resid_send(p).wait_send()
         for p in range(7):
-            resid_send(p).wait_send()
             col_send(p).wait_send()
-        for k in range(3):
-            for p in range(4):
-                single_send(p, k).wait_send()
-
-    @pl.when(relays)
-    def _():
-        for k in range(3):
-            single_send(3, k).wait_send()
+
+    for role, copies in tree:
+
+        @pl.when(role)
+        def _():
+            for k in range(3):
+                for p in copies:
+                    single_send(p, k).wait_send()
 
     @pl.when(not_main)
     def _():
@@ -681,7 +745,9 @@
 def update_kernel(pair, row, col, atom, single, new_pair, atom_out, single_out, result, sem):
     small = [
         pltpu.make_async_copy(atom, atom_out, sem.at[0]),
-        pltpu.make_async_copy(single, single_out, sem.at[1]),
+    ] + [
+        pltpu.make_async_copy(single.at[q], single_out.at[:, pl.ds(q * CH, CH)], sem.at[1 + q])
+        for q in range(3)
     ]
     for copy in small:
         copy.start()
@@ -690,7 +756,7 @@
 
     def out_copy(k):
         rows = pl.ds(k * BLOCK, BLOCK)
-        return pltpu.make_async_copy(result.at[rows], new_pair.at[rows], sem.at[2 + k])
+        return pltpu.make_async_copy(result.at[rows], new_pair.at[rows], sem.at[4 + k])
 
     @pl.loop(0, TOK // BLOCK)
     def _(k):
@@ -720,7 +786,7 @@
         exchange_kernel,
         out_shape=(
             jax.ShapeDtypeStruct((OWN, CH), BF16),
-            jax.ShapeDtypeStruct((TOK, 3 * CH), BF16),
+            jax.ShapeDtypeStruct((3, TOK, CH), BF16),
             jax.ShapeDtypeStruct((TOK, CH), F32),
             jax.ShapeDtypeStruct((2 * TOK, CH), BF16),
         ),
@@ -744,6 +810,7 @@
             vmem((ATOMS, CH), F32),
             vmem((ATOMS, CH), BF16),
             vmem((ATOMS, CH), BF16),
+            vmem((2 * OWN, CH), BF16),
             vmem((OWN, CH), BF16),
             vmem((ATOMS, CH), BF16),
             vmem((ATOMS, 3 * CH), BF16),
@@ -751,9 +818,9 @@
             pltpu.SemaphoreType.DMA((TOK // STEP,)),
             pltpu.SemaphoreType.DMA((2,)),
             pltpu.SemaphoreType.DMA((1 + len(weights),)),
-            pltpu.SemaphoreType.DMA((1,)),
+            pltpu.SemaphoreType.DMA((2,)),
             pltpu.SemaphoreType.DMA((32,)),
-            pltpu.SemaphoreType.DMA((N_COL + 9,)),
+            pltpu.SemaphoreType.DMA((N_COL + 10,)),
         ],
         compiler_params=pltpu.CompilerParams(
             collective_id=0, has_side_effects=True, vmem_limit_bytes=40 * 2**20
@@ -764,13 +831,13 @@
         out_shape=(
             jax.ShapeDtypeStruct(pair.shape, BF16),
             jax.ShapeDtypeStruct(atom.shape, BF16),
-            jax.ShapeDtypeStruct(single.shape, BF16),
+            jax.ShapeDtypeStruct((TOK, 3 * CH), BF16),
         ),
         in_specs=[in_vmem] * 5,
         out_specs=(any_,) * 3,
         scratch_shapes=[
             vmem(pair.shape, BF16),
-            pltpu.SemaphoreType.DMA((2 + TOK // BLOCK,)),
+            pltpu.SemaphoreType.DMA((4 + TOK // BLOCK,)),
         ],
         compiler_params=pltpu.CompilerParams(vmem_limit_bytes=UPDATE_VMEM * 2**20),
     )(pltpu.with_memory_space_constraint(pair, pltpu.VMEM), row, col, atom, single)

time: 32.7 us -> 29 us (0.89)
  Pallas kernels: 31.9 us -> 28.2 us
    pallas_call x1, Pallas kernels: 28.4 us -> 24.7 us  [shards(): pl.pallas_call(exchange_kernel, out_shape=(jax.ShapeDtypeStruct((OWN, CH)...]
where the time goes in v4:
time: 29 us; the launch traced here: 28.9 us
  Pallas kernels  28.2 us (97%)
  between operations  0.66 us (2%)
    pallas_call x1, Pallas kernels, shards(): pl.pallas_call(exchange_kernel, out_shape=(jax.ShapeDtypeStruct((OWN, CH)...  24.7 us
    pallas_call x1, Pallas kernels, shards(): pl.pallas_call(update_kernel, out_shape=(jax.ShapeDtypeStruct(pair.shape,...  3.55 us

profile of v4, /device:TPU:18, one launch (start us, length us, event | category | flops | bytes accessed | tf_op | source)
XLA Modules:
  0.0 28.9 jit_solution(1469115546566072531)
XLA Ops:
  0.6 0.0 copy-start
  0.6 24.7 %shard_map.130 = (bf16[128,128]{1,0:T(8,128)(2,1)S(1)}, bf16[3,128,128]{2,1,0:T(8,128)(2,1)S(1)}, f32[128,128]{1,0:T(8,128)S(1)}, bf16[256,128]{1,0:T(8,128)(2,1)S(1)}) custom-call(bf16[128,256,128]{2,1,0:T(8,128)(2,1)} %pair.1, bf16[128,128]{1,0:T(8,128)(2,1)} %atom_hbm.1, s32[16,128]{1,0:T(8,128)} %counts_hbm.1, f32[4,128]{1,0:T(4,128)} %bitcast.1, ...), custom_call_target="tpu_custom_call" | custom-call | tf_op jit(solution)/shard_map/pallas_call | solution.py:785
  25.3 0.0 copy-done
  25.4 3.6 %shard_map.131 = (bf16[128,256,128]{2,1,0:T(8,128)(2,1)}, bf16[128,128]{1,0:T(8,128)(2,1)}, bf16[128,384]{1,0:T(8,128)(2,1)}) custom-call(bf16[128,256,128]{2,1,0:T(8,128)(2,1)S(1)} %copy-done, f32[128,128]{1,0:T(8,128)S(1)} %get-tuple-element.10.row, bf16[256,128]{1,0:T(8,128)(2,1)S(1)} %get-tuple-element.11.col, ...), custom_call_target="tpu_custom_call" | custom-call | tf_op jit(solution)/shard_map/pallas_call | solution.py:829
Async XLA Ops:
  0.6 24.7 %copy-start = (bf16[128,256,128]{2,1,0:T(8,128)(2,1)S(1)}, bf16[128,256,128]{2,1,0:T(8,128)(2,1)}, u32[]{:S(2)}) copy-start(bf16[128,256,128]{2,1,0:T(8,128)(2,1)} %pair.1) | copy-start | bytes 25165828

commit v5 on v4

--- a/solution.py
+++ b/solution.py
@@ -120,7 +120,6 @@
     sibling = r + 1 - 2 * odd
     partner = c + 1 - 2 * x_hi
     home_side = x_hi == x_lo
-    col_main = 2 * c + odd
     row_peers = [
         (lax.rem(z + dz, 4) * 2 + (1 - x_hi if dx else x_hi))
         for dz, dx in ((2, 1), (1, 1), (3, 1), (2, 0), (0, 1), (1, 0), (3, 0))
@@ -184,8 +183,6 @@
     ahead_of_home = lax.rem(z - y + 4, 4)
     relays = not_main & ((home_side & (ahead_of_home != 2)) | (across & (ahead_of_home == 0)))
     passes_atoms = not_main & home_side
-    feeder = jnp.where(home_side, lax.rem(z + 3, 4), lax.rem(z + 2, 4)) * 2 + x_hi
-
     @pl.when(is_main)
     def _():
         for col in row_peers:
@@ -202,28 +199,19 @@
     @pl.when(not_main)
     def _():
         hello(r, home)
-        hello(col_main, c)
-
-    hello(sibling, c)
-
-    @pl.when(across & (ahead_of_home != 0))
-    def _():
-        hello(r, partner)
-
-    @pl.when(ahead_of_home == 2)
-    def _():
-        hello(r, feeder)
+
+    for n in range(2):
+
+        @pl.when(r != 2 * c + n)
+        def _():
+            hello(2 * c + n, c)
 
     def one(flag):
         return jnp.where(flag, 1, 0)
 
     greetings = (
-        1
-        + one(is_main) * 2 * 7
+        one(is_main) * (N_COL - 1 + N_ROW - 1)
         + one(not_main)
-        + one(passes_atoms)
-        + one(ahead_of_home == 1) * one(home_side)
-        + one(ahead_of_home == 0) * one(across)
         + one(to_next)
         + one(to_prev)
     )

time: 29 us -> 29 us (level)
  no operation moved by 1% of the time
where the time goes in v5:
time: 29 us; the launch traced here: 28.9 us
  Pallas kernels  28.3 us (98%)
  between operations  0.66 us (2%)
    pallas_call x1, Pallas kernels, shards(): pl.pallas_call(exchange_kernel, out_shape=(jax.ShapeDtypeStruct((OWN, CH)...  24.7 us
    pallas_call x1, Pallas kernels, shards(): pl.pallas_call(update_kernel, out_shape=(jax.ShapeDtypeStruct(pair.shape,...  3.55 us

profile of v5, /device:TPU:18, one launch (start us, length us, event | category | flops | bytes accessed | tf_op | source)
XLA Modules:
  0.0 28.9 jit_solution(9899866226961511942)
XLA Ops:
  0.6 0.0 copy-start
  0.6 24.7 %shard_map.130 = (bf16[128,128]{1,0:T(8,128)(2,1)S(1)}, bf16[3,128,128]{2,1,0:T(8,128)(2,1)S(1)}, f32[128,128]{1,0:T(8,128)S(1)}, bf16[256,128]{1,0:T(8,128)(2,1)S(1)}) custom-call(bf16[128,256,128]{2,1,0:T(8,128)(2,1)} %pair.1, bf16[128,128]{1,0:T(8,128)(2,1)} %atom_hbm.1, s32[16,128]{1,0:T(8,128)} %counts_hbm.1, f32[4,128]{1,0:T(4,128)} %bitcast.1, ...), custom_call_target="tpu_custom_call" | custom-call | tf_op jit(solution)/shard_map/pallas_call | solution.py:773
  25.4 0.0 copy-done
  25.4 3.6 %shard_map.131 = (bf16[128,256,128]{2,1,0:T(8,128)(2,1)}, bf16[128,128]{1,0:T(8,128)(2,1)}, bf16[128,384]{1,0:T(8,128)(2,1)}) custom-call(bf16[128,256,128]{2,1,0:T(8,128)(2,1)S(1)} %copy-done, f32[128,128]{1,0:T(8,128)S(1)} %get-tuple-element.10.row, bf16[256,128]{1,0:T(8,128)(2,1)S(1)} %get-tuple-element.11.col, ...), custom_call_target="tpu_custom_call" | custom-call | tf_op jit(solution)/shard_map/pallas_call | solution.py:817
Async XLA Ops:
  0.6 24.7 %copy-start = (bf16[128,256,128]{2,1,0:T(8,128)(2,1)S(1)}, bf16[128,256,128]{2,1,0:T(8,128)(2,1)}, u32[]{:S(2)}) copy-start(bf16[128,256,128]{2,1,0:T(8,128)(2,1)} %pair.1) | copy-start | bytes 25165828

commit v6 on v5

--- a/solution.py
+++ b/solution.py
@@ -329,13 +329,6 @@
         hidden = swish * (0.5 + 0.5 * jnp.tanh(0.5 * swish)) * doubled[:, 2 * CH :]
         return (residual + mm(hidden.astype(BF16), wt[...])).astype(BF16)
 
-    @pl.when(is_helper)
-    def _():
-        weights[0].wait()
-        side_moments(bias_weights())
-        for h, value in enumerate(head_bias(8 * TOK, HALF)):
-            side[h] = value
-
     @pl.when(not_main)
     def _():
         mine.wait()
@@ -349,6 +342,12 @@
     @pl.when(to_prev & not_main)
     def _():
         edge_copy(False, r - 1).start()
+
+    @pl.when(is_helper)
+    def _():
+        weights[0].wait()
+        side_moments(bias_weights())
+        side[...] = jnp.concatenate(head_bias(8 * TOK, HALF), axis=0).astype(BF16)
 
     @pl.when(is_helper)
     def _():
@@ -523,18 +522,42 @@
         for col in [c] + near_first[:EARLY]:
             project(col)
 
+        for col in near_first[EARLY:]:
+            atom_copy(col).wait_recv()
+
+        @pl.when(has_prev)
+        def _():
+            edge_copy(True, r).wait_recv()
+
+        @pl.when(jnp.logical_not(has_prev))
+        def _():
+            atoms[0:MARGIN, :] = jnp.zeros((MARGIN, CH), BF16)
+
+        @pl.when(has_next)
+        def _():
+            edge_copy(False, r).wait_recv()
+
+        @pl.when(jnp.logical_not(has_next))
+        def _():
+            atoms[MARGIN + ATOMS :, :] = jnp.zeros((MARGIN, CH), BF16)
+
         @pl.when(has_helper)
         def _():
             side_copy().wait_recv()
 
         @pl.when(jnp.logical_not(has_helper))
         def _():
-            side_in[...] = jnp.zeros(side_in.shape, F32)
-
-        low_lanes = iota((HALF, TOK), 1) < SPLIT
+            side_in[...] = jnp.zeros(side_in.shape, BF16)
+
+        for col in near_first[EARLY:]:
+            project(col)
+        keys_values(0, MARGIN)
+        keys_values(MARGIN + ATOMS, MARGIN)
+
+        helped = side_in[...].astype(F32)
         mask_lane = iota((TOK, TOK), 1) == MASK_LANE
         for h in range(HEADS):
-            theirs = side_in[h]
+            theirs = helped[h * HALF : (h + 1) * HALF]
             ahead = jnp.where(on_main_next, main_side[h], theirs)
             behind = jnp.where(on_main_next, theirs, main_side[h])
             ahead_rolled = pltpu.roll(ahead, SPLIT, 1)
@@ -552,30 +575,6 @@
                 for w in range(2):
                     start = ((2 * k + w) * HEADS + h) * WIN
                     picked_side[start : start + WIN, :] = rows[w * WIN : (w + 1) * WIN]
-
-        for col in near_first[EARLY:]:
-            atom_copy(col).wait_recv()
-
-        @pl.when(has_prev)
-        def _():
-            edge_copy(True, r).wait_recv()
-
-        @pl.when(jnp.logical_not(has_prev))
-        def _():
-            atoms[0:MARGIN, :] = jnp.zeros((MARGIN, CH), BF16)
-
-        @pl.when(has_next)
-        def _():
-            edge_copy(False, r).wait_recv()
-
-        @pl.when(jnp.logical_not(has_next))
-        def _():
-            atoms[MARGIN + ATOMS :, :] = jnp.zeros((MARGIN, CH), BF16)
-
-        for col in near_first[EARLY:]:
-            project(col)
-        keys_values(0, MARGIN)
-        keys_values(MARGIN + ATOMS, MARGIN)
 
         head_of = iota((WIN, CH), 1) // (CH // HEADS)
 
@@ -785,10 +784,10 @@
             vmem((HALF, TOK, CH), BF16),
             vmem(counts.shape, jnp.int32),
             *[vmem(w.shape, w.dtype) for w in weights],
-            vmem((8 * (TOK + HALF), TOK), F32),
-            vmem((8 * (TOK + HALF), TOK), F32),
-            vmem((HEADS, HALF, TOK), F32),
-            vmem((HEADS, HALF, TOK), F32),
+            vmem((8 * (TOK + HALF + 1), TOK), F32),
+            vmem((8 * (TOK + HALF + 1), TOK), F32),
+            vmem((HEADS * HALF, TOK), BF16),
+            vmem((HEADS * HALF, TOK), BF16),
             vmem((EXT, CH), BF16),
             vmem((ATOMS, CH), BF16),
             vmem((ATOMS * HEADS, TOK), BF16),

time: 29 us -> 29.2 us (level)
  no operation moved by 1% of the time
where the time goes in v6:
time: 29.2 us; the launch traced here: 29 us
  Pallas kernels  28.4 us (97%)
  between operations  0.66 us (2%)
    pallas_call x1, Pallas kernels, shards(): pl.pallas_call(exchange_kernel, out_shape=(jax.ShapeDtypeStruct((OWN, CH)...  24.8 us
    pallas_call x1, Pallas kernels, shards(): pl.pallas_call(update_kernel, out_shape=(jax.ShapeDtypeStruct(pair.shape,...  3.55 us

profile of v6, /device:TPU:18, one launch (start us, length us, event | category | flops | bytes accessed | tf_op | source)
XLA Modules:
  0.0 29.0 jit_solution(3550932881665169253)
XLA Ops:
  0.6 0.0 copy-start
  0.6 24.8 %shard_map.130 = (bf16[128,128]{1,0:T(8,128)(2,1)S(1)}, bf16[3,128,128]{2,1,0:T(8,128)(2,1)S(1)}, f32[128,128]{1,0:T(8,128)S(1)}, bf16[256,128]{1,0:T(8,128)(2,1)S(1)}) custom-call(bf16[128,256,128]{2,1,0:T(8,128)(2,1)} %pair.1, bf16[128,128]{1,0:T(8,128)(2,1)} %atom_hbm.1, s32[16,128]{1,0:T(8,128)} %counts_hbm.1, f32[4,128]{1,0:T(4,128)} %bitcast.1, ...), custom_call_target="tpu_custom_call" | custom-call | tf_op jit(solution)/shard_map/pallas_call | solution.py:772
  25.5 0.0 copy-done
  25.5 3.6 %shard_map.131 = (bf16[128,256,128]{2,1,0:T(8,128)(2,1)}, bf16[128,128]{1,0:T(8,128)(2,1)}, bf16[128,384]{1,0:T(8,128)(2,1)}) custom-call(bf16[128,256,128]{2,1,0:T(8,128)(2,1)S(1)} %copy-done, f32[128,128]{1,0:T(8,128)S(1)} %get-tuple-element.10.row, bf16[256,128]{1,0:T(8,128)(2,1)S(1)} %get-tuple-element.11.col, ...), custom_call_target="tpu_custom_call" | custom-call | tf_op jit(solution)/shard_map/pallas_call | solution.py:816
Async XLA Ops:
  0.6 24.8 %copy-start = (bf16[128,256,128]{2,1,0:T(8,128)(2,1)S(1)}, bf16[128,256,128]{2,1,0:T(8,128)(2,1)}, u32[]{:S(2)}) copy-start(bf16[128,256,128]{2,1,0:T(8,128)(2,1)} %pair.1) | copy-start | bytes 25165828

commit v7 on v6

--- a/solution.py
+++ b/solution.py
@@ -23,9 +23,10 @@
 STEP = 16
 BLOCK = 8
 UPDATE_VMEM = 20
+PARTS = 2
 REACH = 80
 HALF = REACH // 2
-EARLY = 4
+EARLY = 6
 EDGES = (0, 1, 30, 31)
 MASK_LANE = 56
 ATTEND_UNROLL = 28
@@ -170,7 +171,6 @@
         atom_hbm, atoms.at[pl.ds(MARGIN + c * OWN, OWN)], local_sem.at[0]
     )
     mine = pltpu.make_async_copy(atom_hbm, mine_in, local_sem.at[1])
-    mine.start()
     barrier = pltpu.get_barrier_semaphore()
 
     def hello(row, col):
@@ -209,6 +209,7 @@
     def one(flag):
         return jnp.where(flag, 1, 0)
 
+    mine.start()
     greetings = (
         one(is_main) * (N_COL - 1 + N_ROW - 1)
         + one(not_main)
@@ -384,18 +385,18 @@
             resid_in.at[pl.ds(pl.multiple_of((1 - x_hi) * OWN, OWN), OWN)],
             atom_out,
             8,
-            base + 6,
+            base + 1,
             r,
             partner,
         )
 
     def single_send(p, k):
-        piece = single_out.at[k]
+        piece = single_out.at[k // PARTS, pl.ds(k % PARTS * (TOK // PARTS), TOK // PARTS)]
         col = (row_peers[5], row_peers[6], partner, row_peers[3])[p]
-        return send(piece, piece, 12 + 4 * k + p, base + (1, 4, 5)[k], r, col)
+        return send(piece, piece, 12 + 4 * k + p, base + 6 + k, r, col)
 
     tree = (
-        (is_main, (0, 1, 2)),
+        (is_main, (2, 0, 1)),
         (home_side & (ahead_of_home == 1), (0, 2)),
         (home_side & (ahead_of_home == 3), (2,)),
         (across & (ahead_of_home == 0), (3,)),
@@ -404,10 +405,10 @@
     own_half = col_out.at[pl.ds(pl.multiple_of(odd * TOK, TOK), TOK)]
 
     def col_send(p):
-        return send(own_half, own_half, 24 + p, base + 2, col_peers[p], c)
+        return send(own_half, own_half, 12 + 12 * PARTS + p, base + 2, col_peers[p], c)
 
     def col_forward():
-        return send(own_half, own_half, 31, base + 3, sibling, c)
+        return send(own_half, own_half, 9, base + 3, sibling, c)
 
     @pl.when(is_main)
     def _():
@@ -641,8 +642,9 @@
             totals = mm(member[...], emitted[:, part])
             single = (totals / counts_column).astype(BF16)
             single_out[q] = single
-            for p in tree[0][1]:
-                single_send(p, q).start()
+            for k in range(q * PARTS, (q + 1) * PARTS):
+                for p in tree[0][1]:
+                    single_send(p, k).start()
             terms = terms + mm(single, wc[part, :])
         col_out[pl.ds(pl.multiple_of(odd * TOK, TOK), TOK), :] = terms.astype(BF16)
         for p in range(7):
@@ -673,7 +675,7 @@
 
         @pl.when(role)
         def _():
-            for k in range(3):
+            for k in range(3 * PARTS):
                 single_send(0, k).wait_recv()
                 for p in copies:
                     single_send(p, k).start()
@@ -686,7 +688,7 @@
 
     @pl.when(not_main & jnp.logical_not(relays))
     def _():
-        for k in range(3):
+        for k in range(3 * PARTS):
             single_send(0, k).wait_recv()
 
     row_out[...] = sum(mm(single_out[q], wr[q * CH : (q + 1) * CH, :]) for q in range(3))
@@ -712,7 +714,7 @@
 
         @pl.when(role)
         def _():
-            for k in range(3):
+            for k in range(3 * PARTS):
                 for p in copies:
                     single_send(p, k).wait_send()
 
@@ -806,8 +808,8 @@
             pltpu.SemaphoreType.DMA((2,)),
             pltpu.SemaphoreType.DMA((1 + len(weights),)),
             pltpu.SemaphoreType.DMA((2,)),
-            pltpu.SemaphoreType.DMA((32,)),
-            pltpu.SemaphoreType.DMA((N_COL + 10,)),
+            pltpu.SemaphoreType.DMA((12 + 12 * PARTS + 7,)),
+            pltpu.SemaphoreType.DMA((N_COL + 9 + 3 * PARTS,)),
         ],
         compiler_params=pltpu.CompilerParams(
             collective_id=0, has_side_effects=True, vmem_limit_bytes=40 * 2**20

time: 29.2 us -> 28.9 us (0.990)
  no operation moved by 1% of the time
where the time goes in v7:
time: 28.9 us; the launch traced here: 28.8 us
  Pallas kernels  28.2 us (98%)
  between operations  0.66 us (2%)
    pallas_call x1, Pallas kernels, shards(): pl.pallas_call(exchange_kernel, out_shape=(jax.ShapeDtypeStruct((OWN, CH)...  24.6 us
    pallas_call x1, Pallas kernels, shards(): pl.pallas_call(update_kernel, out_shape=(jax.ShapeDtypeStruct(pair.shape,...  3.55 us

profile of v7, /device:TPU:18, one launch (start us, length us, event | category | flops | bytes accessed | tf_op | source)
XLA Modules:
  0.0 28.8 jit_solution(18118618027839397301)
XLA Ops:
  0.6 0.0 copy-start
  0.6 24.6 %shard_map.130 = (bf16[128,128]{1,0:T(8,128)(2,1)S(1)}, bf16[3,128,128]{2,1,0:T(8,128)(2,1)S(1)}, f32[128,128]{1,0:T(8,128)S(1)}, bf16[256,128]{1,0:T(8,128)(2,1)S(1)}) custom-call(bf16[128,256,128]{2,1,0:T(8,128)(2,1)} %pair.1, bf16[128,128]{1,0:T(8,128)(2,1)} %atom_hbm.1, s32[16,128]{1,0:T(8,128)} %counts_hbm.1, f32[4,128]{1,0:T(4,128)} %bitcast.1, ...), custom_call_target="tpu_custom_call" | custom-call | tf_op jit(solution)/shard_map/pallas_call | solution.py:774
  25.3 0.0 copy-done
  25.3 3.6 %shard_map.131 = (bf16[128,256,128]{2,1,0:T(8,128)(2,1)}, bf16[128,128]{1,0:T(8,128)(2,1)}, bf16[128,384]{1,0:T(8,128)(2,1)}) custom-call(bf16[128,256,128]{2,1,0:T(8,128)(2,1)S(1)} %copy-done, f32[128,128]{1,0:T(8,128)S(1)} %get-tuple-element.10.row, bf16[256,128]{1,0:T(8,128)(2,1)S(1)} %get-tuple-element.11.col, ...), custom_call_target="tpu_custom_call" | custom-call | tf_op jit(solution)/shard_map/pallas_call | solution.py:818
Async XLA Ops:
  0.6 24.6 %copy-start = (bf16[128,256,128]{2,1,0:T(8,128)(2,1)S(1)}, bf16[128,256,128]{2,1,0:T(8,128)(2,1)}, u32[]{:S(2)}) copy-start(bf16[128,256,128]{2,1,0:T(8,128)(2,1)} %pair.1) | copy-start | bytes 25165828
